TPU v7x, 32 devices: a whole 2x2x4 slice. The times are simulated.
32 devices in a mesh: dp: 16 (over z, y, x), rows: 2 (over core).
Axes of the slice: x: 2, y: 2, z: 4, core: 2. Of those that a mesh axis runs over, the one named last changes fastest.
Arguments:
- images: bfloat16 [512, 8, 7, 2048], P('dp', 'rows'), may hold values from -6 to 6
- row_split: int32 [512], P('dp'), may hold values from 3 to 4
- labels: int32 [512], P('dp'), may hold values from 0 to 999
- partners: int32 [512], replicated, may hold values from 0 to 511
- image_weight: int32 [512], replicated, may hold values from 1 to 7
- owner_slot: int32 [2176], replicated, may hold values from 0 to 2175, each once
- conv_master: float32 [2176, 4096], P('dp'), may hold values from -0.125 to 0.125
- conv_stats: float32 [2176, 64, 128], P('dp')
- conv_roots: float32 [2176, 64, 128], P('dp')
- head_master: float32 [2048, 1000], P('dp'), may hold values from -0.25 to 0.25
- head_moment_one: float32 [2048, 1000], P('dp'), may hold values from -0.0008544922 to 0.0008544922
- head_moment_two: float32 [2048, 1000], P('dp'), may hold values from 1.315e-08 to 5.26e-08
- small_params: float32 [13288], replicated
- small_moment_one: float32 [13288], replicated, may hold values from -0.0034179688 to 0.0034179688
- small_moment_two: float32 [13288], replicated, may hold values from 2.104e-07 to 8.416e-07
Outputs:
- loss_sum: float32 [], replicated
- weight_total: float32 [], replicated
- conv_grad: float32 [2176, 4096], P('dp')
- conv_stats_new: float32 [2176, 64, 128], P('dp')
- conv_master_new: float32 [2176, 4096], P('dp')
- conv_copy: bfloat16 [2176, 4096], P('dp')
- head_moment_one_new: float32 [2048, 1000], P('dp')
- head_moment_two_new: float32 [2048, 1000], P('dp')
- head_master_new: float32 [2048, 1000], P('dp')
- head_copy: bfloat16 [2048, 1000], P('dp')
- small_moment_one_new: float32 [13288], replicated
- small_moment_two_new: float32 [13288], replicated
- small_params_new: float32 [13288], replicated
Inputs may be any that keep to these rules, and one draw needn't show every extreme that they name: Image i's first row_split[i] rows lie on the first index of rows, right-aligned in its slots, the others on the second, left-aligned. `owner_slot`: a permutation of the 2176 blocks.
All inputs are finite; a program needn't handle non-finite values.
Results may differ from a plain program's by a relative error of at most 0.02.
Values may be sent and summed in bfloat16 or wider, within the bound.
A program may use at most 320 MiB of HBM per device.

v0:
```python
import functools

import jax
import jax.numpy as jnp
import numpy as np
from jax import lax
from jax.experimental import pallas as pl
from jax.experimental.pallas import tpu as pltpu
from jax.sharding import PartitionSpec as P

C = 2048
M = 512
CLASSES = 1000
HEIGHT = 7
WIDTH = 7
ROW_SLOTS = 4
LAYERS = 2
BLOCK = 64
STEP = 5


EPS_NORM = 1e-05
MATCH_WEIGHT = 4.0
DECAY_STATS = 0.5
RATE_SHAMPOO = 0.15
RATE_HEAD = 0.03
RATE_SMALL = 0.2
BETA_FIRST = 0.9
BETA_SECOND = 0.95
EPS_ADAM = 1e-08
DECAY_WEIGHT = 0.01


C = 2048
M = 512
CLASSES = 1000
HEIGHT = 7
WIDTH = 7
ROW_SLOTS = 4
LAYERS = 2
BLOCK = 64
STEP = 5


EPS_NORM = 1e-05
MATCH_WEIGHT = 4.0
DECAY_STATS = 0.5
RATE_SHAMPOO = 0.15
RATE_HEAD = 0.03
RATE_SMALL = 0.2
BETA_FIRST = 0.9
BETA_SECOND = 0.95
EPS_ADAM = 1e-08
DECAY_WEIGHT = 0.01


MESH_IDS = pl.DeviceIdType.MESH
HALF = 16
LANES = 128


def bit_split(devices):
    bits = devices.bit_length() - 1
    first = bits // 3
    second = (bits - first) // 2
    return first, second, bits - first - second


def greet(peers):
    barrier = pltpu.get_barrier_semaphore()
    for peer in peers:
        pl.semaphore_signal(barrier, inc=1, device_id=peer, device_id_type=MESH_IDS)
    pl.semaphore_wait(barrier, len(peers))


def axis_masks(devices, core):
    first, second, third = bit_split(devices)
    low = [m for m in range(1, 1 << first)]
    high = [m << first for m in range(1, 1 << second)]
    if first == second:
        one = [jnp.where(core == 0, h, l) for h, l in zip(high, low)]
        two = [jnp.where(core == 0, l, h) for h, l in zip(high, low)]
    else:
        one, two = low, high
    far = [m << (first + second) for m in range(1, 1 << third)]
    return [0] + one, [0] + two, [0] + far


def even_spans(count):
    parts = 8 if count % 8 == 0 else 1
    return [(i * (count // parts), count // parts) for i in range(parts)]


def spans_of(count):
    spans, at = [], 0
    while at < count:
        rest = count - at
        size = 16 if rest > 8 else rest
        spans.append((at, size))
        at += size
    return spans


def slab_shape(shape):
    return (shape[1] // LANES, shape[0], LANES)


def matrix_list():
    shapes = []
    for _ in range(LAYERS):
        shapes += [(C, M), (9 * M, M), (M, C)]
    return shapes


BRING_LATE = 2


def bring_kernel(devices, spans, idx_ref, m_ref, *refs):
    shapes = matrix_list()
    n = len(shapes)
    outs, bufs, (g_ref, stage, send_sem, recv_sem, out_sem) = refs[:n], refs[n : 2 * n], refs[2 * n :]
    me = lax.axis_index("dp")
    core = lax.axis_index("rows")
    count = m_ref.shape[0]
    parts = len(spans)
    mid, last, far = axis_masks(devices, core)
    partner = (me, 1 - core)
    peers = [(me ^ m, core) for m in far[1:] + mid[1:] + last[1:]] + [partner]
    barrier = pltpu.get_barrier_semaphore()
    for peer in peers:
        pl.semaphore_signal(barrier, inc=1, device_id=peer, device_id_type=MESH_IDS)

    def spread(first, rows):
        for m in range(HALF):
            one = m_ref[pl.ds(first, rows), m * LANES : (m + 1) * LANES]
            two = m_ref[pl.ds(first, rows), (HALF + m) * LANES : (HALF + m + 1) * LANES]
            h, r = m // (HALF // 2), 2 * (m % (HALF // 2))
            for i in range(2):
                cut = slice(i * BLOCK, (i + 1) * BLOCK)
                stage[h, pl.ds(first * HALF + r + i, rows, stride=HALF)] = jnp.concatenate(
                    [one[:, cut], two[:, cut]], axis=1
                )

    def group(i, carry):
        spread(pl.multiple_of(i * 8, 8), 8)
        return carry

    lax.fori_loop(0, count // 8, group, 0)
    if count % 8:
        spread(count // 8 * 8, count % 8)

    def round_one(k, carry):
        for h in range(2):
            rows = pl.ds(pl.multiple_of(k * HALF, HALF), HALF)
            g_ref[(me * 2 + h) * count + k] = stage[h, rows].astype(jnp.bfloat16)
        return carry

    lax.fori_loop(0, count, round_one, 0)
    pl.semaphore_wait(barrier, len(peers))
    sent = []

    def piece(owner, half, part):
        first, size = spans[part]
        return g_ref.at[pl.ds((owner * 2 + half) * count + first, size)]

    def send(owner, part, device):
        copy = pltpu.make_async_remote_copy(
            src_ref=piece(owner, core, part),
            dst_ref=piece(owner, core, part),
            send_sem=send_sem.at[len(sent)],
            recv_sem=recv_sem.at[owner, core, part],
            device_id=device,
            device_id_type=MESH_IDS,
        )
        copy.start()
        sent.append(copy)

    def arrived(owner, half, part):
        ref = piece(owner, half, part)
        pltpu.make_async_copy(ref, ref, recv_sem.at[owner, half, part]).wait()

    def onward(owner, part, masks):
        arrived(owner, core, part)
        for m in masks:
            send(owner, part, (me ^ m, core))
        send(owner, part, partner)

    early = parts - BRING_LATE if parts > BRING_LATE else parts
    for part in range(parts):
        order = far[1:] + last[1:] + mid[1:] if part < early else mid[1:] + far[1:] + last[1:]
        for m in order:
            send(me, part, (me ^ m, core))
    for tick in range(parts + 2):
        part = tick
        if part < parts:
            if part < early:
                for z in far[1:]:
                    onward(me ^ z, part, last[1:] + mid[1:])
            else:
                for m in mid[1:]:
                    onward(me ^ m, part, far[1:] + last[1:])
        part = tick - 1
        if 0 <= part < parts:
            if part < early:
                for m in mid[1:]:
                    for z in far:
                        onward(me ^ m ^ z, part, last[1:])
            else:
                for z in far[1:]:
                    onward(me ^ z, part, last[1:])
                for z in far[1:]:
                    for m in mid[1:]:
                        onward(me ^ z ^ m, part, last[1:])
        part = tick - 2
        if 0 <= part < parts:
            for q in last[1:]:
                for z in far:
                    for m in mid:
                        onward(me ^ q ^ z ^ m, part, [])
    for step in range(1, devices):
        for part in range(parts):
            arrived(me ^ step, 1 - core, part)

    base = 0
    copies = []
    for at, (rows, cols) in enumerate(shapes):
        pairs = cols // LANES
        buf = bufs[at]

        def strip(r, carry, base=base, pairs=pairs, buf=buf):
            for m in range(pairs):
                even = idx_ref[base + r * (2 * pairs) + 2 * m]
                odd = idx_ref[base + r * (2 * pairs) + 2 * m + 1]
                for h in range(2):
                    e = g_ref[even + h * count]
                    o = g_ref[odd + h * count]
                    buf[m, pl.ds(r * BLOCK + h * HALF, HALF)] = jnp.concatenate(
                        [e[:, :BLOCK], o[:, :BLOCK]], axis=1
                    )
                    buf[m, pl.ds(r * BLOCK + 2 * HALF + h * HALF, HALF)] = jnp.concatenate(
                        [e[:, BLOCK:], o[:, BLOCK:]], axis=1
                    )
            return carry

        lax.fori_loop(0, rows // BLOCK, strip, 0, unroll=8 // (pairs // 4))
        copy = pltpu.make_async_copy(buf, outs[at], out_sem.at[at])
        copy.start()
        copies.append(copy)
        base += (rows // BLOCK) * (cols // BLOCK)
    for copy in copies:
        copy.wait()
    for copy in sent:
        copy.wait_send()


def bring_weights(master, index, devices):
    count = master.shape[0]
    spans = even_spans(count)
    parts = len(spans)
    shapes = [slab_shape(s) for s in matrix_list()]
    dma = pltpu.SemaphoreType.DMA
    return pl.pallas_call(
        functools.partial(bring_kernel, devices, spans),
        out_shape=[jax.ShapeDtypeStruct(s, jnp.bfloat16) for s in shapes],
        in_specs=[
            pl.BlockSpec(memory_space=pltpu.SMEM),
            pl.BlockSpec(memory_space=pltpu.VMEM),
        ],
        out_specs=[pl.BlockSpec(memory_space=pl.ANY)] * len(shapes),
        scratch_shapes=[pltpu.VMEM(s, jnp.bfloat16) for s in shapes]
        + [
            pltpu.VMEM((devices * 2 * count, HALF, LANES), jnp.bfloat16),
            pltpu.VMEM((2, count * HALF, LANES), jnp.float32),
            dma((3 * devices * parts,)),
            dma((devices, 2, parts)),
            dma((len(shapes),)),
        ],
        compiler_params=pltpu.CompilerParams(
            collective_id=1, has_side_effects=True, vmem_limit_bytes=56 * 2**20
        ),
    )(index, master)


def split_two(v):
    high = v.astype(BF16)
    return high, (v - high.astype(F32)).astype(BF16)


def shampoo_rows(final, master, stats, roots, grads, flat, turn, first, group):
    for k in range(group):
        rows = pl.ds(k * HALF, HALF)
        parts = [final[h, first + k].astype(F32) for h in range(2)]
        for h in range(2):
            flat[h, rows] = parts[h]
        tile = jnp.concatenate([p[:, :BLOCK] for p in parts] + [p[:, BLOCK:] for p in parts], axis=0)
        low = tile.astype(BF16)
        old = stats[first + k]
        sides = roots[first + k]
        high, rest = split_two(sides[:, :BLOCK])
        both = dot(jnp.concatenate([high, rest, tile.T.astype(BF16)], axis=0), low, 1, 0)
        stats[first + k] = DECAY_STATS * old + (1.0 - DECAY_STATS) * jnp.concatenate(
            [dot(low, low, 1, 1), both[2 * BLOCK :]], axis=1
        )
        turned = both[:BLOCK] + both[BLOCK : 2 * BLOCK]
        t_high, t_rest = split_two(turned)
        high, rest = split_two(sides)
        wide = jnp.concatenate([high[:, BLOCK:], rest[:, BLOCK:]], axis=1)
        both = dot(jnp.concatenate([t_high, t_rest], axis=0), wide, 1, 0)
        turned = both[:BLOCK, :BLOCK] + both[BLOCK:, :BLOCK] + both[:BLOCK, BLOCK:]
        for h in range(2):
            turn[h, rows] = jnp.concatenate(
                [
                    turned[h * HALF : (h + 1) * HALF],
                    turned[2 * HALF + h * HALF : 2 * HALF + (h + 1) * HALF],
                ],
                axis=1,
            )
    here = pl.ds(first if isinstance(first, int) else pl.multiple_of(first, 8), group)
    for m in range(HALF):
        h, r = m // (HALF // 2), 2 * (m % (HALF // 2))
        tiles = [flat[h, pl.ds(r + i, group, stride=HALF)] for i in range(2)]
        steps = [turn[h, pl.ds(r + i, group, stride=HALF)] for i in range(2)]
        for p in range(2):
            lanes = pl.ds(p * (BLOCK * BLOCK // 2) + m * LANES, LANES)
            cut = slice(p * BLOCK, (p + 1) * BLOCK)
            grads[here, lanes] = jnp.concatenate([v[:, cut] for v in tiles], axis=1)
            master[here, lanes] = master[here, lanes] - RATE_SHAMPOO * jnp.concatenate(
                [v[:, cut] for v in steps], axis=1
            )


DELIVER_FAR = ()
AHEAD = 3


def deliver_kernel(devices, spans, code_ref, head_h, *refs):
    n = len(matrix_list())
    grads, refs = refs[:n], refs[n:]
    master_h, stats_h, roots_h, head_out, grad_out, stats_out, master_out = refs[:7]
    pool, acc, land_last, land_mid, land_far, final = refs[7:13]
    master, stats, roots, grad_flat, flat, turn = refs[13:19]
    in_sem, send_sem, last_recv, mid_recv, far_recv, end_send, end_recv, own_sem, out_sem = refs[19:]
    me = lax.axis_index("dp")
    core = lax.axis_index("rows")
    count = code_ref.shape[0] // devices
    mid, last, far = axis_masks(devices, core)
    partner = (me, 1 - core)
    peers = [(me ^ m, core) for m in far[1:] + mid[1:] + last[1:]] + [partner]
    barrier = pltpu.get_barrier_semaphore()
    for peer in peers:
        pl.semaphore_signal(barrier, inc=1, device_id=peer, device_id_type=MESH_IDS)
    head = pltpu.make_async_copy(
        head_h, acc.at[:, pl.ds(count, head_h.shape[1])], in_sem.at[n]
    )
    head.start()
    loads = []
    start = 0
    for i, grad in enumerate(grads):
        load = pltpu.make_async_copy(grad, pool.at[pl.ds(start, grad.shape[0])], in_sem.at[i])
        load.start()
        loads.append(load)
        start += grad.shape[0]
    owned = []
    for i, (src, dst) in enumerate([(stats_h, stats), (roots_h, roots), (master_h, master)]):
        load = pltpu.make_async_copy(src, dst, own_sem.at[i])
        load.start()
        owned.append(load)
    pl.semaphore_wait(barrier, len(peers))
    head.wait()
    sent = []
    stores = []

    def store(src, dst):
        copy = pltpu.make_async_copy(src, dst, out_sem.at[len(stores)])
        copy.start()
        stores.append(copy)

    def send(owner, span, part, land, sems, at, device):
        copy = pltpu.make_async_remote_copy(
            src_ref=acc.at[owner, span],
            dst_ref=land.at[at, span],
            send_sem=send_sem.at[len(sent)],
            recv_sem=sems.at[at, part],
            device_id=device,
            device_id_type=MESH_IDS,
        )
        copy.start()
        sent.append(copy)

    def arrived(land, sems, at, span, part):
        ref = land.at[at, span]
        pltpu.make_async_copy(ref, ref, sems.at[at, part]).wait()

    def fill(first, size):
        def owner_step(owner, carry):
            def block(k, inner):
                slot = owner * count + first + k
                code = code_ref[slot]
                q = lax.shift_right_logical(code, 1)
                top = pool[q]
                low = pool[q + 1]
                even = jnp.concatenate([top[:, :BLOCK], low[:, :BLOCK]], axis=1)
                odd = jnp.concatenate([top[:, BLOCK:], low[:, BLOCK:]], axis=1)
                acc[owner, first + k] = jnp.where(lax.bitwise_and(code, 1) == 1, odd, even)
                return inner

            return lax.fori_loop(0, size, block, carry, unroll=True)

        lax.fori_loop(0, devices, owner_step, 0)

    def add(owners, lands, first, size):
        def step(i, carry):
            at = first + i
            for owner, (land, j) in zip(owners, lands):
                acc[owner, at] = (
                    acc[owner, at].astype(jnp.float32) + land[j, at].astype(jnp.float32)
                ).astype(jnp.bfloat16)
            return carry

        lax.fori_loop(0, size, step, 0)

    ends = []
    parts = len(spans)
    whole_rows = master.shape[0] % 8 != 0

    def far_second(part):
        return part in DELIVER_FAR

    for tick in range(parts + 3 + AHEAD):
        part = tick
        if part < parts:
            first, size = spans[part]
            span = pl.ds(first, size)
            if part == 1:
                for load in loads:
                    load.wait()
            if part > 0:
                fill(first, size)
            at = 0
            for q in last[1:]:
                for m in mid[::-1]:
                    for z in far[::-1]:
                        send(
                            me ^ q ^ m ^ z, span, part, land_last, last_recv, at, (me ^ q, core)
                        )
                        at += 1
        part = tick - AHEAD
        if 0 <= part < parts:
            first, size = spans[part]
            span = pl.ds(first, size)
            pairs = [(m, z) for m in mid[::-1] for z in far[::-1]]
            owners, lands = [], []
            for j in range(len(last) - 1):
                for i, (m, z) in enumerate(pairs):
                    at = j * len(pairs) + i
                    arrived(land_last, last_recv, at, span, part)
                    owners.append(me ^ m ^ z)
                    lands.append((land_last, at))
            add(owners, lands, first, size)
            at = 0
            if far_second(part):
                for z in far[1:]:
                    for m in mid[::-1]:
                        send(me ^ m ^ z, span, part, land_far, far_recv, at, (me ^ z, core))
                        at += 1
            else:
                for m in mid[1:]:
                    for z in far[::-1]:
                        send(me ^ m ^ z, span, part, land_mid, mid_recv, at, (me ^ m, core))
                        at += 1
        part = tick - 1 - AHEAD
        if 0 <= part < parts:
            first, size = spans[part]
            span = pl.ds(first, size)
            owners, lands = [], []
            at = 0
            if far_second(part):
                for z in far[1:]:
                    for m in mid[::-1]:
                        arrived(land_far, far_recv, at, span, part)
                        owners.append(me ^ m)
                        lands.append((land_far, at))
                        at += 1
                add(owners, lands, first, size)
                for at, m in enumerate(mid[1:]):
                    send(me ^ m, span, part, land_mid, mid_recv, at, (me ^ m, core))
            else:
                for m in mid[1:]:
                    for z in far[::-1]:
                        arrived(land_mid, mid_recv, at, span, part)
                        owners.append(me ^ z)
                        lands.append((land_mid, at))
                        at += 1
                add(owners, lands, first, size)
                for at, z in enumerate(far[1:]):
                    send(me ^ z, span, part, land_far, far_recv, at, (me ^ z, core))
        part = tick - 2 - AHEAD
        if 0 <= part < parts:
            first, size = spans[part]
            span = pl.ds(first, size)
            land, sems, width = land_far, far_recv, len(far) - 1
            if far_second(part):
                land, sems, width = land_mid, mid_recv, len(mid) - 1
            for at in range(width):
                arrived(land, sems, at, span, part)

            def finish(i, carry, first=first, land=land, width=width):
                at = first + i
                total = acc[me, at].astype(jnp.float32)
                for j in range(width):
                    total = total + land[j, at].astype(jnp.float32)
                final[core, at] = total.astype(jnp.bfloat16)
                return carry

            lax.fori_loop(0, size, finish, 0)
            copy = pltpu.make_async_remote_copy(
                src_ref=final.at[core, span],
                dst_ref=final.at[core, span],
                send_sem=end_send.at[part],
                recv_sem=end_recv.at[part],
                device_id=partner,
                device_id_type=MESH_IDS,
            )
            copy.start()
            ends.append(copy)
        part = tick - 3 - AHEAD
        if 0 <= part < parts:
            first, size = spans[part]
            ref = final.at[1 - core, pl.ds(first, size)]
            pltpu.make_async_copy(ref, ref, end_recv.at[part]).wait()
            if part == 0:
                store(final.at[:, pl.ds(first, size)], head_out)
                for load in owned:
                    load.wait()
                continue

            def group(i, carry, first=first):
                shampoo_rows(final, master, stats, roots, grad_flat, flat, turn, first + i * 8, 8)
                return carry

            lax.fori_loop(0, size // 8, group, 0)
            if size % 8:
                shampoo_rows(
                    final, master, stats, roots, grad_flat, flat, turn, first + size // 8 * 8, size % 8
                )
            span = pl.ds(first, size)
            store(stats.at[span], stats_out.at[span])
            if not whole_rows:
                store(grad_flat.at[span], grad_out.at[span])
                store(master.at[span], master_out.at[span])
    if whole_rows:
        store(grad_flat, grad_out)
        store(master, master_out)
    for copy in sent + ends:
        copy.wait_send()
    for copy in stores:
        copy.wait()


def deliver_blocks(grads, head, code, master, stats, roots, devices):
    count = code.shape[0] // devices
    more = head.shape[1]
    spans = [(count, more)] + spans_of(count)
    first, second, third = bit_split(devices)
    n_mid, n_last, n_far = 1 << first, 1 << second, 1 << third
    tile = (count + more, HALF, LANES)
    dma = pltpu.SemaphoreType.DMA
    lands = [(n_last - 1) * n_mid * n_far, (n_mid - 1) * n_far, (n_far - 1) * n_mid]
    grads = [g.reshape(-1, HALF, LANES) for g in grads]
    any_space = pl.BlockSpec(memory_space=pl.ANY)
    steps = len(spans)
    return pl.pallas_call(
        functools.partial(deliver_kernel, devices, spans),
        out_shape=[
            jax.ShapeDtypeStruct((2, more, HALF, LANES), BF16),
            jax.ShapeDtypeStruct(master.shape, F32),
            jax.ShapeDtypeStruct(stats.shape, F32),
            jax.ShapeDtypeStruct(master.shape, F32),
        ],
        in_specs=[pl.BlockSpec(memory_space=pltpu.SMEM)] + [any_space] * (4 + len(grads)),
        out_specs=[any_space] * 4,
        scratch_shapes=[
            pltpu.VMEM((sum(g.shape[0] for g in grads), HALF, LANES), jnp.bfloat16),
            pltpu.VMEM((devices,) + tile, jnp.bfloat16),
        ]
        + [pltpu.VMEM((k,) + tile, jnp.bfloat16) for k in lands]
        + [
            pltpu.VMEM((2,) + tile, jnp.bfloat16),
            pltpu.VMEM(master.shape, F32),
            pltpu.VMEM(stats.shape, F32),
            pltpu.VMEM(roots.shape, F32),
            pltpu.VMEM(master.shape, F32),
            pltpu.VMEM((2, 8 * HALF, LANES), F32),
            pltpu.VMEM((2, 8 * HALF, LANES), F32),
            dma((len(grads) + 1,)),
            dma((sum(lands) * steps,)),
            dma((lands[0], steps)),
            dma((lands[1], steps)),
            dma((lands[2], steps)),
            dma((steps,)),
            dma((steps,)),
            dma((3,)),
            dma((3 * steps,)),
        ],
        compiler_params=pltpu.CompilerParams(
            collective_id=2, has_side_effects=True, vmem_limit_bytes=60 * 2**20
        ),
    )(code, head, *grads, master, stats, roots)


def block_places(owner_slot):
    codes = []
    base = 0
    for rows, cols in matrix_list():
        strips, pairs = rows // BLOCK, cols // LANES
        grid = base + 2 * (np.arange(pairs)[None, :] * strips + np.arange(strips)[:, None])
        codes.append((2 * grid[:, :, None] + np.arange(2)[None, None, :]).reshape(-1))
        base += 2 * strips * pairs
    code = np.concatenate(codes).astype(np.int32)
    slots = np.arange(code.shape[0], dtype=np.int32)
    found = jnp.sum(
        jnp.where(owner_slot[:, None] == slots[None, :], code[:, None], 0), axis=0, dtype=jnp.int32
    )
    return found


ROWS = ROW_SLOTS * WIDTH
N_IN = C // LANES
N_MID = M // LANES
WIDE = 1024
F32 = jnp.float32
BF16 = jnp.bfloat16


def dot(a, b, ca, cb):
    return lax.dot_general(a, b, (((ca,), (cb,)), ((), ())), preferred_element_type=F32)


def lanes_of(ref, first, count):
    return jnp.concatenate([ref[first + i] for i in range(count)], axis=-1)


def half_tanh(v):
    return 0.5 * (1.0 + jnp.tanh(0.5 * v))


class Net:
    def __init__(self, devices):
        first, second, third = bit_split(devices)
        self.me = lax.axis_index("dp")
        self.core = lax.axis_index("rows")
        self.near, self.far = 1 << (first + second), 1 << third
        self.near_at = lax.rem(self.me, self.near)
        self.far_at = self.me // self.near
        self.partner = (self.me, 1 - self.core)
        self.near_peers = [(self.me ^ m, self.core) for m in range(1, self.near)]
        self.near_slots = [self.near_at ^ m for m in range(1, self.near)]
        self.far_peers = [(self.me ^ (m * self.near), self.core) for m in range(1, self.far)]
        self.far_slots = [self.far_at ^ m for m in range(1, self.far)]

    def hello(self):
        barrier = pltpu.get_barrier_semaphore()
        for peer in [self.partner] + self.near_peers + self.far_peers:
            pl.semaphore_signal(barrier, inc=1, device_id=peer, device_id_type=MESH_IDS)

    def ready(self):
        pl.semaphore_wait(
            pltpu.get_barrier_semaphore(), 1 + len(self.near_peers) + len(self.far_peers)
        )


def slots_total(devices):
    first, second, third = bit_split(devices)
    return 2 + (1 << (first + second)) + (1 << third)


def remote(src, dst, send_sem, recv_sem, device):
    copy = pltpu.make_async_remote_copy(
        src_ref=src,
        dst_ref=dst,
        send_sem=send_sem,
        recv_sem=recv_sem,
        device_id=device,
        device_id_type=MESH_IDS,
    )
    copy.start()
    return copy


def landed(ref, sem):
    pltpu.make_async_copy(ref, ref, sem).wait()


def plain_sum(values, counts):
    total = values[0]
    for value in values[1:]:
        total = total + value
    return total


def pooled_moments(rows):
    def merge(values, counts):
        n = counts[0]
        for more in counts[1:]:
            n = n + more
        sums = values[0][:rows]
        spread = values[0][rows:]
        for value in values[1:]:
            sums = sums + value[:rows]
            spread = spread + value[rows:]
        mean = sums / n
        for value, own in zip(values, counts):
            gap = value[:rows] / own - mean
            spread = spread + own * gap * gap
        return jnp.concatenate([sums, spread], axis=0)

    return merge


def reduce_all(net, value, bufs, send_sem, recv_sem, merge, own_count=None, pair_count=0.0, fillers=()):
    fillers = list(fillers) + [None] * 3
    copies = []
    stages = [
        (0, net.core, [net.partner], [1 - net.core], 2),
        (2, net.near_at, net.near_peers, net.near_slots, net.near),
        (2 + net.near, net.far_at, net.far_peers, net.far_slots, net.far),
    ]
    for step, (base, mine, peers, slots, size) in enumerate(stages):
        bufs[base + mine] = value
        for i, peer in enumerate(peers):
            copies.append(
                remote(
                    bufs.at[base + mine],
                    bufs.at[base + mine],
                    send_sem.at[base + i],
                    recv_sem.at[base + mine],
                    peer,
                )
            )
        if fillers[step] is not None:
            fillers[step]()
        for slot in slots:
            landed(bufs.at[base + slot], recv_sem.at[base + slot])
        if own_count is None:
            counts = [None] * size
        elif step == 0:
            rest = pair_count - own_count
            first = net.core == 0
            counts = [jnp.where(first, own_count, rest), jnp.where(first, rest, own_count)]
        else:
            counts = [pair_count * (1 if step == 1 else net.near)] * size
        value = merge([bufs[base + j] for j in range(size)], counts)
    return value, copies


def column_sum(value):
    return jnp.sum(value.reshape(-1, 8, LANES), axis=0)


def local_moments(z, count, live, own_count, stage, masked):
    quarter = z.shape[1] // 4

    def slab(j, carry):
        total = jnp.zeros((8, LANES), F32)
        for q in range(4):
            rows = pl.ds(q * quarter, quarter)
            v = z[j, rows]
            if masked:
                v = v * live[rows]
                z[j, rows] = v
            total = total + column_sum(v)
        sums = jnp.sum(total, axis=0, keepdims=True)
        mean = sums / own_count
        spread = jnp.zeros((8, LANES), F32)
        for q in range(4):
            rows = pl.ds(q * quarter, quarter)
            d = (z[j, rows] - mean) * live[rows]
            spread = spread + column_sum(d * d)
        stage[pl.ds(j, 1)] = sums
        stage[pl.ds(count + j, 1)] = jnp.sum(spread, axis=0, keepdims=True)
        return carry

    lax.fori_loop(0, count, slab, 0)


def window(ref, down, right):
    batch = ref.shape[3]
    parts = [
        ref[j, pl.ds(down, ROW_SLOTS), pl.ds(right, WIDTH)].reshape(ROWS * batch, LANES)
        for j in range(N_MID)
    ]
    return jnp.concatenate(parts, axis=-1)


def clear_edges(ref, core):
    shape = ref.shape
    zero = jnp.zeros((shape[0], 1) + shape[2:], ref.dtype)
    ref[:, pl.ds(jnp.where(core == 0, 0, ROW_SLOTS + 1), 1)] = zero
    column = jnp.zeros(shape[:2] + (1,) + shape[3:], ref.dtype)
    ref[:, :, 0:1] = column
    ref[:, :, WIDTH + 1 : WIDTH + 2] = column


def send_edge(ref, net, send_sem, recv_sem):
    edge = jnp.where(net.core == 0, ROW_SLOTS, 1)
    there = jnp.where(net.core == 0, 0, ROW_SLOTS + 1)
    return remote(
        ref.at[:, edge, pl.ds(1, WIDTH)],
        ref.at[:, there, pl.ds(1, WIDTH)],
        send_sem,
        recv_sem,
        net.partner,
    )


def edge_landed(ref, net, recv_sem):
    here = jnp.where(net.core == 0, ROW_SLOTS + 1, 0)
    landed(ref.at[:, here, pl.ds(1, WIDTH)], recv_sem)


def edge_first(net, fill, send):
    edge = jnp.where(net.core == 0, ROW_SLOTS - 1, 0)
    fill(edge)
    copy = send()
    for step in range(1, ROW_SLOTS):
        fill(lax.rem(edge + step, ROW_SLOTS))
    return copy


def load_all(pairs, sems):
    copies = []
    for i, (src, dst) in enumerate(pairs):
        copy = pltpu.make_async_copy(src, dst, sems.at[i])
        copy.start()
        copies.append(copy)
    return copies


def forward_kernel(devices, top, total_count, *refs):
    refs = list(refs)
    take = lambda n: [refs.pop(0) for _ in range(n)]
    xb_h, xf_h = take(2) if top else [None, None]
    wi_h, wm_h, wo_h = take(3)
    if not top:
        xb, = take(1)
    params, live = take(2)
    za_h, hp_h, zb_h, hb_h, zc_h, stat_a, stat_b, stat_c = take(8)
    if top:
        pooled, = take(1)
    else:
        xn_h, xnb_h = take(2)
    if top:
        xb, xf = take(2)
    wi, wm, wo, za, hp, zb, hb, zc = take(8)
    if not top:
        xn, xnb = take(2)
    stage_m, stage_c, buf_a, buf_b, buf_c = take(5)
    in_sem, out_sem, send_sem, recv_sem, halo_sem = take(5)

    net = Net(devices)
    net.hello()
    loads = load_all(
        [(wi_h, wi), (wm_h, wm), (wo_h, wo)] + ([(xb_h, xb), (xf_h, xf)] if top else []), in_sem
    )
    clear_edges(hp, net.core)
    zb[...] = jnp.zeros(zb.shape, F32)
    own_count = jnp.sum(column_sum(live[...]), axis=0, keepdims=True)
    pair_count = total_count / devices
    quarter = za.shape[1] // ROW_SLOTS
    batch = quarter // WIDTH
    stores = []
    sends = []

    def store(src, dst):
        copy = pltpu.make_async_copy(src, dst, out_sem.at[len(stores)])
        copy.start()
        stores.append(copy)

    def norm(z, n, stage, bufs, which, masked, stat):
        local_moments(z, n, live, own_count, stage, masked)
        if which == 0:
            net.ready()
        total, copies = reduce_all(
            net,
            stage[...],
            bufs,
            send_sem.at[which],
            recv_sem.at[which],
            pooled_moments(n),
            own_count,
            pair_count,
        )
        sends.extend(copies)
        stat[0:n] = total[:n] / total_count
        stat[n : 2 * n] = lax.rsqrt(total[n:] / total_count + EPS_NORM)

    def affine(stat, n, gain_at, j):
        mean = stat[pl.ds(j, 1)]
        scale = stat[pl.ds(n + j, 1)] * params[pl.ds(gain_at + j, 1)]
        return mean, scale, params[pl.ds(gain_at + n + j, 1)]

    loads[0].wait()
    if top:
        loads[3].wait()
    product = dot(lanes_of(xb, 0, N_IN) if top else xb[...], lanes_of(wi, 0, N_MID), 1, 0)
    for j in range(N_MID):
        za[j] = product[:, j * LANES : (j + 1) * LANES]
    norm(za, N_MID, stage_m, buf_a, 0, not top, stat_a)
    store(za, za_h)

    def fill_hidden(slot):
        rows = pl.ds(slot * quarter, quarter)

        def slab(j, carry):
            mean, scale, shift = affine(stat_a, N_MID, 0, j)
            y = (za[j, rows] - mean) * scale + shift
            h = (live[rows] * (y * half_tanh(y))).astype(BF16)
            hp[j, pl.ds(slot + 1, 1), pl.ds(1, WIDTH)] = h.reshape(1, WIDTH, batch, LANES)
            return carry

        lax.fori_loop(0, N_MID, slab, 0)

    sends.append(
        edge_first(net, fill_hidden, lambda: send_edge(hp, net, halo_sem.at[0], halo_sem.at[1]))
    )
    loads[1].wait()

    def tap(t):
        k = pl.ds(pl.multiple_of(t * M, M), M)
        part = dot(
            window(hp, t // 3, lax.rem(t, 3)),
            jnp.concatenate([wm[j, k] for j in range(N_MID)], axis=-1),
            1,
            0,
        )
        for j in range(N_MID):
            zb[j] = zb[j] + part[:, j * LANES : (j + 1) * LANES]

    def middle(i, carry):
        tap(i + 3)
        return carry

    def outer(i, carry):
        tap(jnp.where(i < 3, i, i + 3))
        return carry

    lax.fori_loop(0, 3, middle, 0)
    edge_landed(hp, net, halo_sem.at[1])
    store(hp, hp_h)
    lax.fori_loop(0, 6, outer, 0)
    norm(zb, N_MID, stage_m, buf_b, 1, True, stat_b)
    store(zb, zb_h)

    def fill_second(j, carry):
        mean, scale, shift = affine(stat_b, N_MID, 2 * N_MID, j)
        for q in range(4):
            rows = pl.ds(q * quarter, quarter)
            y = (zb[j, rows] - mean) * scale + shift
            hb[j, rows] = (live[rows] * (y * half_tanh(y))).astype(BF16)
        return carry

    lax.fori_loop(0, N_MID, fill_second, 0)
    store(hb, hb_h)
    loads[2].wait()

    def expand(g, carry):
        part = dot(lanes_of(hb, 0, N_MID), lanes_of(wo, g * N_MID, N_MID), 1, 0)
        for j in range(N_MID):
            zc[g * N_MID + j] = part[:, j * LANES : (j + 1) * LANES]
        return carry

    lax.fori_loop(0, N_IN // N_MID, expand, 0)
    store(zc, zc_h)
    norm(zc, N_IN, stage_c, buf_c, 2, False, stat_c)
    if top:
        loads[4].wait()

    def finish(j, carry):
        mean, scale, shift = affine(stat_c, N_IN, 4 * N_MID, j)
        pool = jnp.zeros((batch, LANES), F32)
        for q in range(4):
            rows = pl.ds(q * quarter, quarter)
            if top:
                x = xf[j, rows]
            else:
                x = xb[rows, pl.ds(pl.multiple_of(j * LANES, LANES), LANES)].astype(F32)
            y = (zc[j, rows] - mean) * scale + shift + x
            out = live[rows] * (y * half_tanh(y))
            if top:
                pool = pool + jnp.sum(out.reshape(WIDTH, batch, LANES), axis=0)
            else:
                xn[j, rows] = out
                xnb[j, rows] = out.astype(BF16)
        if top:
            pooled[j] = pool
        return carry

    lax.fori_loop(0, N_IN, finish, 0)
    if not top:
        store(xn, xn_h)
        store(xnb, xnb_h)
    for copy in stores:
        copy.wait()
    for copy in sends:
        copy.wait_send()


def forward_layer(devices, top, total_count, ident, xb, xf, weights, params, live):
    rows = live.shape[0]
    batch = rows // ROWS
    shape = jax.ShapeDtypeStruct
    any_space = pl.BlockSpec(memory_space=pl.ANY)
    vmem = pl.BlockSpec(memory_space=pltpu.VMEM)
    fields = [
        shape((N_MID, rows, LANES), F32),
        shape((N_MID, ROW_SLOTS + 2, WIDTH + 2, batch, LANES), BF16),
        shape((N_MID, rows, LANES), F32),
        shape((N_MID, rows, LANES), BF16),
        shape((N_IN, rows, LANES), F32),
    ]
    stats = [shape((2 * n, LANES), F32) for n in (N_MID, N_MID, N_IN)]
    if top:
        last = [shape((N_IN, batch, LANES), F32)]
        last_specs = [vmem]
    else:
        last = [shape((N_IN, rows, LANES), F32), shape((N_IN, rows, LANES), BF16)]
        last_specs = [any_space] * 2
    big = lambda s: pltpu.VMEM(s.shape, s.dtype)
    total = slots_total(devices)
    dma = pltpu.SemaphoreType.DMA
    ins = ([xb, xf] if top else []) + list(weights)
    small_ins = ([] if top else [xb]) + [params, live]
    return pl.pallas_call(
        functools.partial(forward_kernel, devices, top, total_count),
        out_shape=fields + stats + last,
        in_specs=[any_space] * len(ins) + [vmem] * len(small_ins),
        out_specs=[any_space] * 5 + [vmem] * 3 + last_specs,
        scratch_shapes=[big(a) for a in ins]
        + [big(s) for s in fields]
        + ([] if top else [big(s) for s in last])
        + [
            pltpu.VMEM((2 * N_MID, LANES), F32),
            pltpu.VMEM((2 * N_IN, LANES), F32),
            pltpu.VMEM((total, 2 * N_MID, LANES), F32),
            pltpu.VMEM((total, 2 * N_MID, LANES), F32),
            pltpu.VMEM((total, 2 * N_IN, LANES), F32),
            dma((5,)),
            dma((8,)),
            dma((3, total)),
            dma((3, total)),
            dma((2,)),
        ],
        compiler_params=pltpu.CompilerParams(
            collective_id=ident, has_side_effects=True, vmem_limit_bytes=60 * 2**20
        ),
    )(*ins, *small_ins)


def head_kernel(
    devices, area, pooled, head_h, bias, pick, point, numbers, hot,
    extra, gtop, gh_h,
    head, send_pool, recv_pool, low, logits_all, logits, g_low, gh, gh_there, gh_other, gt,
    in_sem, out_sem, send_sem, recv_sem,
):
    net = Net(devices)
    net.hello()
    load = pltpu.make_async_copy(head_h, head, in_sem)
    load.start()
    half = send_pool.shape[1]
    mine = pl.ds(pl.multiple_of(net.core * half, half), half)
    theirs = pl.ds(pl.multiple_of((1 - net.core) * half, half), half)
    for j in range(N_IN):
        send_pool[j] = pooled[j, theirs].astype(BF16)
    net.ready()
    sends = [remote(send_pool, recv_pool, send_sem.at[0], recv_sem.at[0], net.partner)]
    load.wait()
    landed(recv_pool, recv_sem.at[0])
    for j in range(N_IN):
        low[j] = ((pooled[j, mine] + recv_pool[j].astype(F32)) / area).astype(BF16)
    logits[...] = dot(lanes_of(low, 0, N_IN), lanes_of(head, 0, N_IN), 1, 1) + bias[0:1, :]
    logits_all[net.core, net.far_at, net.near_at] = logits[...].astype(BF16)
    at = 1
    ref = logits_all.at[net.core, net.far_at, net.near_at]
    for peer in net.far_peers:
        sends.append(
            remote(ref, ref, send_sem.at[at], recv_sem.at[1 + net.near + net.far_at], peer)
        )
        at += 1

    own = logits[...]
    keep = lax.broadcasted_iota(jnp.int32, own.shape, 1) < CLASSES
    peak = jnp.max(jnp.where(keep, own, -3.0e38), axis=1, keepdims=True)
    powers = jnp.where(keep, jnp.exp(jnp.where(keep, own - peak, 0.0)), 0.0)
    log_total = peak + jnp.log(jnp.sum(powers, axis=1, keepdims=True))
    softmax = jnp.where(keep, jnp.exp(jnp.where(keep, own - log_total, 0.0)), 0.0)
    picked = jnp.sum(own * hot[...], axis=1, keepdims=True)

    for slot in net.far_slots:
        landed(
            logits_all.at[net.core, slot, net.near_at], recv_sem.at[1 + net.near + slot]
        )
    group = logits_all.at[net.core, :, net.near_at]
    for peer in net.near_peers:
        sends.append(remote(group, group, send_sem.at[at], recv_sem.at[1 + net.near_at], peer))
        at += 1
    for slot in net.near_slots:
        landed(logits_all.at[net.core, :, slot], recv_sem.at[1 + slot])
    ref = logits_all.at[net.core]
    sends.append(
        remote(ref, ref, send_sem.at[at], recv_sem.at[1 + net.near + net.far], net.partner)
    )
    at += 1
    landed(logits_all.at[1 - net.core], recv_sem.at[1 + net.near + net.far])
    every = logits_all[...].reshape(-1, WIDE)
    gap = jnp.where(keep, own - dot(pick[...], every, 1, 0), 0.0)
    incoming = dot(point[...], every, 1, 0)
    weight = numbers[:, 0:1]
    terms = weight * (
        log_total - picked + MATCH_WEIGHT * (jnp.sum(gap * gap, axis=1, keepdims=True) / CLASSES)
    )
    grad = (
        weight * (softmax - hot[...])
        + MATCH_WEIGHT
        * (2.0 / CLASSES)
        * (weight * gap - (incoming - numbers[:, 1:2] * own))
    ) / numbers[:, 2:3]
    g_low[...] = jnp.where(keep, grad, 0.0).astype(BF16)
    bias_sum = jnp.sum(g_low[...].astype(F32), axis=0, keepdims=True)
    extra[...] = jnp.zeros(extra.shape, F32)
    for j in range(WIDE // LANES):
        extra[j : j + 1] = bias_sum[:, j * LANES : (j + 1) * LANES]
    extra[WIDE // LANES : WIDE // LANES + 1] = jnp.zeros((1, LANES), F32) + jnp.sum(
        terms, axis=0, keepdims=True
    )
    gt_view = gt.at[:, net.core]
    for j in range(N_IN):
        gt[j, net.core] = (dot(g_low[...], head[j], 1, 0) / area).astype(BF16)
    sends.append(
        remote(
            gt_view, gt_view, send_sem.at[at], recv_sem.at[2 + net.near + net.far], net.partner
        )
    )

    at += 1
    block = (WIDE // 2 // HALF, HALF, LANES)
    cut = WIDE // 2
    mine_at = pl.multiple_of(net.core * cut, cut)
    theirs_at = pl.multiple_of((1 - net.core) * cut, cut)

    def grad_there(j, carry):
        part = dot(g_low[:, pl.ds(theirs_at, cut)], low[j], 0, 0)
        gh_there[j] = part.astype(BF16).reshape(block)
        return carry

    lax.fori_loop(0, N_IN, grad_there, 0)
    sends.append(
        remote(gh_there, gh_other, send_sem.at[at], recv_sem.at[3 + net.near + net.far], net.partner)
    )
    landed(gt.at[:, 1 - net.core], recv_sem.at[2 + net.near + net.far])
    for j in range(N_IN):
        gtop[j] = jnp.concatenate([gt[j, 0], gt[j, 1]], axis=0).astype(F32)
    landed(gh_other, recv_sem.at[3 + net.near + net.far])

    def grad_here(j, carry):
        part = dot(g_low[:, pl.ds(mine_at, cut)], low[j], 0, 0)
        gh[j] = (part.reshape(block) + gh_other[j].astype(F32)).astype(BF16)
        return carry

    lax.fori_loop(0, N_IN, grad_here, 0)
    store = pltpu.make_async_copy(gh, gh_h, out_sem)
    store.start()
    store.wait()
    for copy in sends:
        copy.wait_send()


def head_step(devices, pooled, head, bias, pick, point, numbers, hot):
    batch = pooled.shape[1]
    half = batch // 2
    shape = jax.ShapeDtypeStruct
    any_space = pl.BlockSpec(memory_space=pl.ANY)
    vmem = pl.BlockSpec(memory_space=pltpu.VMEM)
    dma = pltpu.SemaphoreType.DMA
    count = 4 + slots_total(devices)
    first, second, third = bit_split(devices)
    near, far = 1 << (first + second), 1 << third
    return pl.pallas_call(
        functools.partial(head_kernel, devices, float(HEIGHT * WIDTH)),
        out_shape=[
            shape((16, LANES), F32),
            shape((N_IN, batch, LANES), F32),
            shape((N_IN, WIDE // 2 // HALF, HALF, LANES), BF16),
        ],
        in_specs=[vmem, any_space] + [vmem] * 5,
        out_specs=[vmem, vmem, any_space],
        scratch_shapes=[
            pltpu.VMEM((N_IN, WIDE, LANES), BF16),
            pltpu.VMEM((N_IN, half, LANES), BF16),
            pltpu.VMEM((N_IN, half, LANES), BF16),
            pltpu.VMEM((N_IN, half, LANES), BF16),
            pltpu.VMEM((2, far, near, half, WIDE), BF16),
            pltpu.VMEM((half, WIDE), F32),
            pltpu.VMEM((half, WIDE), BF16),
            pltpu.VMEM((N_IN, WIDE // 2 // HALF, HALF, LANES), BF16),
            pltpu.VMEM((N_IN, WIDE // 2 // HALF, HALF, LANES), BF16),
            pltpu.VMEM((N_IN, WIDE // 2 // HALF, HALF, LANES), BF16),
            pltpu.VMEM((N_IN, 2, half, LANES), BF16),
            dma(()),
            dma(()),
            dma((count,)),
            dma((count,)),
        ],
        compiler_params=pltpu.CompilerParams(
            collective_id=5, has_side_effects=True, vmem_limit_bytes=60 * 2**20
        ),
    )(pooled, head, bias, pick, point, numbers, hot)


def pieces(part, j):
    return part[:, j * LANES : (j + 1) * LANES].astype(BF16).reshape(-1, 2, HALF, LANES)


def backward_kernel(devices, top, total_count, *refs):
    refs = list(refs)
    take = lambda n: [refs.pop(0) for _ in range(n)]
    field_h = refs.pop(0)
    xb_h, = take(1) if top else [None]
    zc_h, hb_h, hp_h, zb_h, za_h, wi_h, wm_h, wo_h = take(8)
    if not top:
        xb, = take(1)
    gtop, stat_a, stat_b, stat_c, params, live, extra = take(7)
    gi_h, gm_h, go_h = take(3)
    gout_h, = take(1) if top else [None]
    small, = take(1)
    field = refs.pop(0)
    if top:
        xb, = take(1)
    zc, hb, hp, zb, za, wi, wm, wo = take(8)
    gi, gm, go = take(3)
    ri, rm, ro = take(3)
    ec, ep, ea, ub, ua = take(5)
    stage_m, stage_c, buf_a, buf_b, buf_c = take(5)
    in_sem, out_sem, send_sem, recv_sem, halo_sem, pair_sem = take(6)

    net = Net(devices)
    net.hello()
    loads = load_all(
        [
            (zc_h, zc), (field_h, field), (za_h, za), (wo_h, wo), (zb_h, zb), (hb_h, hb),
            (hp_h, hp), (wm_h, wm), (wi_h, wi),
        ]
        + ([(xb_h, xb)] if top else []),
        in_sem,
    )
    clear_edges(ep, net.core)
    quarter = za.shape[1] // ROW_SLOTS
    batch = quarter // WIDTH
    stores = []
    sends = []

    def store(src, dst):
        copy = pltpu.make_async_copy(src, dst, out_sem.at[len(stores)])
        copy.start()
        stores.append(copy)

    def swap(grad, other, at):
        sends.append(
            remote(
                grad.at[:, :, 1 - net.core], other, pair_sem.at[0, at], pair_sem.at[1, at], net.partner
            )
        )

    def fold(grad, other, at, out):
        landed(other, pair_sem.at[1, at])

        def step(i, carry):
            other[:, i] = (grad[:, i, net.core].astype(F32) + other[:, i].astype(F32)).astype(BF16)
            return carry

        lax.fori_loop(0, grad.shape[1], step, 0)
        store(other, out)

    def slope(y):
        sigma = half_tanh(y)
        return sigma * (1.0 + y * (1.0 - sigma))

    def row(ref, j):
        return ref[pl.ds(j, 1)]

    def totals(stage, bufs, which, small_at, n, fillers=()):
        total, copies = reduce_all(
            net, stage[...], bufs, send_sem.at[which], recv_sem.at[which], plain_sum, fillers=fillers
        )
        sends.extend(copies)
        small[small_at : small_at + 2 * n] = total[: 2 * n]
        return total

    loads[0].wait()
    loads[1].wait()

    def slab_c(j, carry):
        mean, scale = row(stat_c, j), row(stat_c, N_IN + j)
        gain, shift = row(params, 4 * N_MID + j), row(params, 4 * N_MID + N_IN + j)
        total = jnp.zeros((8, LANES), F32)
        crossed = jnp.zeros((8, LANES), F32)
        for q in range(4):
            rows = pl.ds(q * quarter, quarter)
            normed = (zc[j, rows] - mean) * scale
            if top:
                x = field[j, rows]
                g = jnp.concatenate([gtop[j]] * WIDTH, axis=0)
            else:
                x = xb[rows, pl.ds(pl.multiple_of(j * LANES, LANES), LANES)].astype(F32)
                g = field[j, rows]
            u = g * live[rows] * slope(normed * gain + shift + x)
            field[j, rows] = u
            total = total + column_sum(u)
            crossed = crossed + column_sum(u * normed)
        stage_c[pl.ds(j, 1)] = jnp.sum(crossed, axis=0, keepdims=True)
        stage_c[pl.ds(N_IN + j, 1)] = jnp.sum(total, axis=0, keepdims=True)
        return carry

    lax.fori_loop(0, N_IN, slab_c, 0)
    stage_c[2 * N_IN :] = extra[...]
    net.ready()
    total_c = totals(stage_c, buf_c, 2, 4 * N_MID, N_IN)
    small[4 * N_MID + 2 * N_IN :] = total_c[2 * N_IN :]

    def back_c(j, carry):
        mean, scale = row(stat_c, j), row(stat_c, N_IN + j)
        gain = row(params, 4 * N_MID + j)
        cross = row(small, 4 * N_MID + j) / total_count
        plain = row(small, 4 * N_MID + N_IN + j) / total_count
        for q in range(4):
            rows = pl.ds(q * quarter, quarter)
            normed = (zc[j, rows] - mean) * scale
            e = live[rows] * ((gain * scale) * (field[j, rows] - plain - normed * cross))
            ec[j, rows] = e.astype(BF16)
        return carry

    lax.fori_loop(0, N_IN, back_c, 0)
    loads[3].wait()
    product = dot(lanes_of(ec, 0, N_IN), lanes_of(wo, 0, N_IN), 1, 1)
    for j in range(N_MID):
        ub[j] = product[:, j * LANES : (j + 1) * LANES]
    loads[4].wait()

    def sums_of(u_ref, z_ref, stat, gain_at, stage):
        def slab(j, carry):
            mean, scale = row(stat, j), row(stat, N_MID + j)
            gain, shift = row(params, gain_at + j), row(params, gain_at + N_MID + j)
            total = jnp.zeros((8, LANES), F32)
            crossed = jnp.zeros((8, LANES), F32)
            for q in range(4):
                rows = pl.ds(q * quarter, quarter)
                normed = (z_ref[j, rows] - mean) * scale
                u = u_ref[j, rows] * live[rows] * slope(normed * gain + shift)
                u_ref[j, rows] = u
                total = total + column_sum(u)
                crossed = crossed + column_sum(u * normed)
            stage[pl.ds(j, 1)] = jnp.sum(crossed, axis=0, keepdims=True)
            stage[pl.ds(N_MID + j, 1)] = jnp.sum(total, axis=0, keepdims=True)
            return carry

        lax.fori_loop(0, N_MID, slab, 0)

    def back_of(u_ref, z_ref, stat, gain_at, small_at, j, rows):
        normed = (z_ref[j, rows] - row(stat, j)) * row(stat, N_MID + j)
        cross = row(small, small_at + j) / total_count
        plain = row(small, small_at + N_MID + j) / total_count
        factor = row(params, gain_at + j) * row(stat, N_MID + j)
        return (live[rows] * (factor * (u_ref[j, rows] - plain - normed * cross))).astype(BF16)

    sums_of(ub, zb, stat_b, 2 * N_MID, stage_m)
    loads[5].wait()

    def grad_out(first, last):
        def group(g, carry):
            part = dot(lanes_of(hb, 0, N_MID), lanes_of(ec, g * N_MID, N_MID), 0, 0)
            for j in range(N_MID):
                go[g * N_MID + j] = pieces(part, j)
            return carry

        return lambda: lax.fori_loop(first, last, group, 0)

    groups = N_IN // N_MID
    totals(
        stage_m, buf_b, 1, 2 * N_MID, N_MID,
        [grad_out(0, 1), grad_out(1, groups - 1), grad_out(groups - 1, groups)],
    )
    swap(go, ro, 0)

    def fill_b(slot):
        rows = pl.ds(slot * quarter, quarter)

        def slab(j, carry):
            e = back_of(ub, zb, stat_b, 2 * N_MID, 2 * N_MID, j, rows)
            ep[j, pl.ds(slot + 1, 1), pl.ds(1, WIDTH)] = e.reshape(1, WIDTH, batch, LANES)
            return carry

        lax.fori_loop(0, N_MID, slab, 0)

    sends.append(
        edge_first(net, fill_b, lambda: send_edge(ep, net, halo_sem.at[0], halo_sem.at[1]))
    )
    loads[6].wait()
    loads[7].wait()
    ua[...] = jnp.zeros(ua.shape, F32)

    def grad_mid(first, last):
        def one(t, carry):
            part = dot(window(hp, t // 3, lax.rem(t, 3)), window(ep, 1, 1), 0, 0)
            for j in range(N_MID):
                gm[j, pl.ds(t * (M // 32), M // 32)] = pieces(part, j)
            return carry

        return lambda: lax.fori_loop(first, last, one, 0)

    def tap(t):
        k = pl.ds(pl.multiple_of(t * M, M), M)
        part = dot(
            window(ep, 2 - t // 3, 2 - lax.rem(t, 3)),
            jnp.concatenate([wm[j, k] for j in range(N_MID)], axis=-1),
            1,
            1,
        )
        for j in range(N_MID):
            ua[j] = ua[j] + part[:, j * LANES : (j + 1) * LANES]

    def middle(i, carry):
        tap(i + 3)
        return carry

    def outer(i, carry):
        tap(jnp.where(i < 3, i, i + 3))
        return carry

    lax.fori_loop(0, 3, middle, 0)
    edge_landed(ep, net, halo_sem.at[1])
    lax.fori_loop(0, 6, outer, 0)
    fold(go, ro, 0, go_h)
    loads[2].wait()
    sums_of(ua, za, stat_a, 0, stage_m)
    totals(
        stage_m, buf_a, 0, 0, N_MID, [grad_mid(0, 2), grad_mid(2, 5), grad_mid(5, 9)]
    )
    swap(gm, rm, 1)

    def fill_a(j, carry):
        for q in range(4):
            rows = pl.ds(q * quarter, quarter)
            ea[j, rows] = back_of(ua, za, stat_a, 0, 0, j, rows)
        return carry

    lax.fori_loop(0, N_MID, fill_a, 0)
    if top:
        loads[9].wait()

    def grad_in(g, carry):
        if top:
            x = lanes_of(xb, g * N_MID, N_MID)
        else:
            x = xb[:, pl.ds(pl.multiple_of(g * M, M), M)]
        part = dot(x, lanes_of(ea, 0, N_MID), 0, 0)
        for j in range(N_MID):
            gi[j, pl.ds(g * (M // 32), M // 32)] = pieces(part, j)
        return carry

    lax.fori_loop(0, groups, grad_in, 0)
    swap(gi, ri, 2)
    loads[8].wait()
    if top:

        def grad_field(g, carry):
            k = pl.ds(pl.multiple_of(g * M, M), M)
            part = dot(
                lanes_of(ea, 0, N_MID),
                jnp.concatenate([wi[j, k] for j in range(N_MID)], axis=-1),
                1,
                1,
            )
            for j in range(N_MID):
                at = g * N_MID + j
                field[at] = field[at] + part[:, j * LANES : (j + 1) * LANES]
            return carry

        lax.fori_loop(0, groups, grad_field, 0)
        store(field, gout_h)
    fold(gm, rm, 1, gm_h)
    fold(gi, ri, 2, gi_h)
    for copy in stores:
        copy.wait()
    for copy in sends:
        copy.wait_send()


def backward_layer(
    devices, top, total_count, ident, field, xb, kept, weights, gtop, params, live, extra
):
    za, hp, zb, hb, zc, stat_a, stat_b, stat_c = kept
    wi, wm, wo = weights
    shape = jax.ShapeDtypeStruct
    any_space = pl.BlockSpec(memory_space=pl.ANY)
    vmem = pl.BlockSpec(memory_space=pltpu.VMEM)
    dma = pltpu.SemaphoreType.DMA
    total = slots_total(devices)
    rows = za.shape[1]
    big = lambda s: pltpu.VMEM(s.shape, s.dtype)
    ins = [field] + ([xb] if top else []) + [zc, hb, hp, zb, za, wi, wm, wo]
    small_ins = ([] if top else [xb]) + [gtop, stat_a, stat_b, stat_c, params, live, extra]
    grads = [shape((w.shape[0], w.shape[1] // 32, HALF, LANES), BF16) for w in weights]
    both = [shape((w.shape[0], w.shape[1] // 32, 2, HALF, LANES), BF16) for w in weights]
    more = [shape(field.shape, F32)] if top else []
    small_rows = 4 * N_MID + 2 * N_IN + extra.shape[0]
    return pl.pallas_call(
        functools.partial(backward_kernel, devices, top, total_count),
        out_shape=grads + more + [shape((small_rows, LANES), F32)],
        in_specs=[any_space] * len(ins) + [vmem] * len(small_ins),
        out_specs=[any_space] * (3 + len(more)) + [vmem],
        scratch_shapes=[big(a) for a in ins]
        + [big(g) for g in both]
        + [big(g) for g in grads]
        + [
            pltpu.VMEM((N_IN, rows, LANES), BF16),
            pltpu.VMEM(hp.shape, BF16),
            pltpu.VMEM((N_MID, rows, LANES), BF16),
            pltpu.VMEM((N_MID, rows, LANES), F32),
            pltpu.VMEM((N_MID, rows, LANES), F32),
            pltpu.VMEM((2 * N_MID, LANES), F32),
            pltpu.VMEM((2 * N_IN + extra.shape[0], LANES), F32),
            pltpu.VMEM((total, 2 * N_MID, LANES), F32),
            pltpu.VMEM((total, 2 * N_MID, LANES), F32),
            pltpu.VMEM((total, 2 * N_IN + extra.shape[0], LANES), F32),
            dma((10,)),
            dma((4,)),
            dma((3, total)),
            dma((3, total)),
            dma((2,)),
            dma((2, 3)),
        ],
        compiler_params=pltpu.CompilerParams(
            collective_id=ident, has_side_effects=True, vmem_limit_bytes=62 * 2**20
        ),
    )(*ins, *small_ins)


def adamw(values_old, gradient, moment_one, moment_two, step_rate):
    one_new = BETA_FIRST * moment_one + (1.0 - BETA_FIRST) * gradient
    two_new = BETA_SECOND * moment_two + (1.0 - BETA_SECOND) * gradient * gradient
    fixed_one = 1.0 - BETA_FIRST**STEP
    fixed_two = 1.0 - BETA_SECOND**STEP
    update = one_new / fixed_one / (jnp.sqrt(two_new / fixed_two) + EPS_ADAM)
    return (one_new, two_new, values_old - step_rate * (update + DECAY_WEIGHT * values_old))


def body(
    images,
    row_split,
    labels,
    partners,
    image_weight,
    owner_slot,
    conv_master,
    conv_stats,
    conv_roots,
    head_master,
    head_moment_one,
    head_moment_two,
    small_params,
    small_moment_one,
    small_moment_two,
):
    devices = lax.axis_size("dp")
    core_index = lax.axis_index("rows")
    batch_size = images.shape[0]
    half_batch = batch_size // 2
    slot_count = images.shape[1]
    total_images = partners.shape[0]
    live_count = float(total_images * HEIGHT * WIDTH)
    owned = conv_master.shape[0]
    head_rows = head_master.shape[0]

    slot_index = (owner_slot // owned) * (2 * owned) + owner_slot % owned
    weights = list(bring_weights(conv_master, slot_index, devices))
    head_t = jnp.pad(head_master.T.astype(BF16), ((0, WIDE - CLASSES), (0, 0)))
    head_t, weights[0] = lax.optimization_barrier((head_t, weights[0]))
    head_all = lax.all_gather(head_t, "dp", axis=0)
    if head_rows != LANES:
        head_all = head_all.transpose(1, 0, 2).reshape(WIDE, N_IN, LANES).transpose(1, 0, 2)

    slot_ids = core_index * slot_count + jnp.arange(slot_count, dtype=jnp.int32)
    first_live = (ROW_SLOTS - row_split)[:, None]
    live = (slot_ids[None, :] >= first_live) & (slot_ids[None, :] < first_live + HEIGHT)
    rows = slot_count * WIDTH * batch_size
    live_rows = jnp.broadcast_to(
        live.T.astype(F32)[:, None, :, None], (slot_count, WIDTH, batch_size, LANES)
    ).reshape(rows, LANES)
    first = images.transpose(1, 2, 0, 3).reshape(rows, C)
    stride = 4 * M + 2 * C
    params = [
        small_params[at * stride : (at + 1) * stride].reshape(-1, LANES) for at in range(LAYERS)
    ]
    bias = jnp.pad(small_params[LAYERS * stride :], (0, WIDE - CLASSES))[None, :]

    kept = []
    field, low = None, first
    lows = []
    for at in range(LAYERS):
        last = at == LAYERS - 1
        lows.append(low)
        out = forward_layer(
            devices,
            at > 0,
            live_count,
            3 + at,
            low,
            field,
            weights[3 * at : 3 * at + 3],
            params[at],
            live_rows,
        )
        kept.append(out[:8])
        if last:
            pooled = out[8]
        else:
            field, low = out[8], out[9]

    def by_core(v):
        return v.reshape(devices, 2, half_batch).transpose(1, 0, 2).reshape(-1)

    weight_f = image_weight.astype(F32)
    weight_total = jnp.sum(weight_f)
    own_start = (lax.axis_index("dp") * 2 + core_index) * half_batch
    own_ids = own_start + jnp.arange(half_batch, dtype=jnp.int32)
    own_weight = lax.dynamic_slice_in_dim(weight_f, own_start, half_batch)
    own_partner = lax.dynamic_slice_in_dim(partners, own_start, half_batch)
    own_label = lax.dynamic_slice_in_dim(labels, core_index * half_batch, half_batch)
    ids = by_core(jnp.arange(total_images, dtype=jnp.int32))
    pick = (own_partner[:, None] == ids[None, :]).astype(BF16)
    point = (by_core(partners)[None, :] == own_ids[:, None]).astype(F32) * by_core(weight_f)[None, :]
    in_weight = jnp.sum(point, axis=1)
    hot = (own_label[:, None] == jnp.arange(WIDE, dtype=jnp.int32)[None, :]).astype(F32)
    lane = jnp.arange(LANES)[None, :]
    numbers = jnp.where(
        lane == 0, own_weight[:, None], jnp.where(lane == 1, in_weight[:, None], weight_total)
    )
    extra, g_top, grad_head = head_step(
        devices,
        pooled,
        head_all,
        bias,
        pick,
        point.astype(BF16),
        numbers,
        hot,
    )
    head_blocks = head_rows // 4
    if head_rows != LANES:
        grad_head = (
            grad_head.reshape(N_IN, WIDE // 2, LANES)
            .transpose(1, 0, 2)
            .reshape(WIDE // 2, devices, head_rows)
            .transpose(1, 0, 2)
            .reshape(devices, head_blocks, HALF, LANES)
        )
    no_extra = jnp.zeros_like(extra)
    top = backward_layer(
        devices, True, live_count, 6, field, lows[1], kept[1], weights[3:], g_top, params[1],
        live_rows, extra,
    )
    bottom = backward_layer(
        devices, False, live_count, 7, top[3], lows[0], kept[0], weights[:3], no_extra, params[0],
        live_rows, no_extra,
    )
    small_top, small_bottom = top[4], bottom[3]
    head_sum, conv_grad, stats_new, master_new = deliver_blocks(
        list(bottom[:3]) + list(top[:3]),
        grad_head,
        block_places(owner_slot),
        conv_master,
        conv_stats,
        conv_roots,
        devices,
    )
    head_grad = head_sum.reshape(WIDE, head_rows)[:CLASSES].T.astype(F32)
    head_one, head_two, head_new = adamw(
        head_master, head_grad, head_moment_one, head_moment_two, RATE_HEAD
    )
    layer_rows = stride // LANES
    grad_bias = small_top[layer_rows : layer_rows + WIDE // LANES].reshape(-1)[:CLASSES]
    loss_sum = small_top[layer_rows + WIDE // LANES, 0]
    grad_small = jnp.concatenate(
        [small_bottom[:layer_rows].reshape(-1), small_top[:layer_rows].reshape(-1), grad_bias]
    )
    small_one, small_two, small_new = adamw(
        small_params, grad_small, small_moment_one, small_moment_two, RATE_SMALL
    )
    return (
        loss_sum,
        weight_total,
        conv_grad,
        stats_new,
        master_new,
        master_new.astype(BF16),
        head_one,
        head_two,
        head_new,
        head_new.astype(BF16),
        small_one,
        small_two,
        small_new,
    )


def solution(mesh):
    in_specs = (
        P("dp", "rows", None, None),
        P("dp"),
        P("dp"),
        P(),
        P(),
        P(),
        P("dp", None),
        P("dp", None, None),
        P("dp", None, None),
        P("dp", None),
        P("dp", None),
        P("dp", None),
        P(),
        P(),
        P(),
    )
    out_specs = (
        P(),
        P(),
        P("dp", None),
        P("dp", None, None),
        P("dp", None),
        P("dp", None),
        P("dp", None),
        P("dp", None),
        P("dp", None),
        P("dp", None),
        P(),
        P(),
        P(),
    )
    return jax.shard_map(body, mesh=mesh, in_specs=in_specs, out_specs=out_specs, check_vma=False)
```

profile of v0, /device:TPU:0, one launch (start us, length us, event | category | flops | bytes accessed | tf_op | source)
XLA Modules:
  0.0 504.6 jit_solution(333989118095627526)
XLA Ops:
  7.2 0.0 copy-start.10
  7.2 0.0 copy-start.11
  7.2 0.0 copy-start.12
  7.2 0.0 all-gather.3.cloned.1.call-start
  7.3 1.3 fusion.5.idx_ref
  8.6 1.1 convert_bitcast_fusion
  9.6 92.3 %shard_map.264 = (bf16[4,2048,128]{2,1,0:T(8,128)(2,1)}, bf16[4,4608,128]{2,1,0:T(8,128)(2,1)}, bf16[16,512,128]{2,1,0:T(8,128)(2,1)}, bf16[4,2048,128]{2,1,0:T(...) custom-call(s32[2176]{0:T(1024)} %fusion.5.idx_ref, f32[136,4096]{1,0:T(8,128)} %refs_6_.1), custom_call_target="tpu_custom_call" | custom-call | tf_op jit(solution)/shard_map/pallas_call | solution.py:262
  101.9 0.7 pad.8
  102.7 0.0 all-gather.3.cloned.1.call-update
  102.7 0.0 copy-done.10
  102.7 0.1 reshape.209
  102.8 0.1 dynamic_slice.10
  102.9 0.0 copy-done.11
  102.9 0.1 reshape.208
  103.0 0.1 dynamic_slice.9
  103.1 0.0 copy-done.12
  103.1 0.1 and_convert_fusion
  103.1 0.1 broadcast_in_dim.78
  103.2 5.9 %copy.35 = bf16[4,7,32,2048]{3,2,1,0:T(8,128)(2,1)} copy(bf16[4,7,32,2048]{3,0,1,2:T(4,128)(2,1)} %bitcast.39) | data formatting | bytes 7340032 | tf_op jit(solution)/shard_map/transpose | solution.py:1598
  109.1 0.1 mul.111
  109.2 0.1 eq.83
  109.3 0.1 reshape.207
  109.4 0.0 copy-done.13
  109.4 0.1 dynamic_slice.11
  109.5 0.6 pad.9
  110.1 0.0 copy-done.5
  110.1 0.6 slice_bitcast_fusion.2
  110.7 1.0 broadcast_in_dim.79.refs_5_.refs_6_.refs_15_
  111.7 52.6 %shard_map.265 = (f32[4,896,128]{2,1,0:T(8,128)}, bf16[4,6,9,32,128]{4,3,2,1,0:T(8,128)(2,1)}, f32[4,896,128]{2,1,0:T(8,128)}, bf16[4,896,128]{2,1,0:T(8,128)(2,...) custom-call(bf16[4,2048,128]{2,1,0:T(8,128)(2,1)} %get-tuple-element, ...), custom_call_target="tpu_custom_call" | custom-call | tf_op jit(solution)/shard_map/pallas_call | solution.py:1033
  164.3 0.0 copy-start.9
  164.3 0.0 copy-start.14
  164.3 47.1 %shard_map.266 = (f32[4,896,128]{2,1,0:T(8,128)}, bf16[4,6,9,32,128]{4,3,2,1,0:T(8,128)(2,1)}, f32[4,896,128]{2,1,0:T(8,128)}, bf16[4,896,128]{2,1,0:T(8,128)(2,...) custom-call(bf16[16,896,128]{2,1,0:T(8,128)(2,1)} %get-tuple-element, ...), custom_call_target="tpu_custom_call" | custom-call | tf_op jit(solution)/shard_map/pallas_call | solution.py:1033
  211.5 0.6 convert_reduce_fusion
  212.1 0.2 select_reduce_fusion.1
  212.2 1.3 select_select_fusion.numbers
  213.6 0.7 compare_convert_fusion.pick
  214.2 0.7 select_convert_fusion.point
  214.9 0.7 fusion.2.hot
  215.6 0.0 copy-done.14
  215.6 3.3 select_reduce_fusion.code_ref
  219.0 33.8 %shard_map.267 = (f32[16,128]{1,0:T(8,128)}, f32[16,32,128]{2,1,0:T(8,128)}, bf16[16,32,16,128]{3,2,1,0:T(8,128)(2,1)}) custom-call(f32[16,32,128]{2,1,0:T(8,128)} %get-tuple-element.70.pooled, bf16[16,1024,128]{2,1,0:T(8,128)(2,1)} %bitcast.38, f32[1,1024]{1,0:T(1,128)} %bitcast.50, bf16[16,512]{1,0:T(8,128)(2,1)} %compare_convert_fusion.pick, ...), custom_call_target="tpu_custom_call" | custom-call | tf_op jit(solution)/shard_map/pallas_call | solution.py:1187
  252.8 60.0 %shard_map.268 = (bf16[4,64,16,128]{3,2,1,0:T(8,128)(2,1)}, bf16[4,144,16,128]{3,2,1,0:T(8,128)(2,1)}, bf16[16,16,16,128]{3,2,1,0:T(8,128)(2,1)}, f32[16,896,128]{2,1,0:T(8,128)}, f32[64,128]{1,0:T(8,128)}) custom-call(f32[16,896,128]{2,1,0:T(8,128)} %get-tuple-element.60.refs_1_.refs_0_, bf16[16,896,128]{2,1,0:T(8,128)(2,1)} %get-tuple-element.61.refs_0_.refs_1_, ...), custom_call_target="tpu_custom_call" | custom-call | tf_op jit(solution)/shard_map/pallas_call | solution.py:1515
  312.9 0.7 slice_bitcast_fusion
  313.6 0.7 slice_bitcast_fusion.4
  314.3 0.6 broadcast_in_dim.89.refs_10_.refs_16_
  314.9 58.0 %shard_map.269 = (bf16[4,64,16,128]{3,2,1,0:T(8,128)(2,1)}, bf16[4,144,16,128]{3,2,1,0:T(8,128)(2,1)}, bf16[16,16,16,128]{3,2,1,0:T(8,128)(2,1)}, f32[64,128]{1,0:T(8,128)}) custom-call(f32[16,896,128]{2,1,0:T(8,128)} %get-tuple-element.79.refs_0_, f32[16,896,128]{2,1,0:T(8,128)} %get-tuple-element.80.refs_1_, ...), custom_call_target="tpu_custom_call" | custom-call | tf_op jit(solution)/shard_map/pallas_call | solution.py:1515
  372.9 0.0 copy-start.3
  372.9 0.0 copy-start.4
  372.9 110.9 %shard_map.270 = (bf16[2,32,16,128]{3,2,1,0:T(8,128)(2,1)}, f32[136,4096]{1,0:T(8,128)}, f32[136,64,128]{2,1,0:T(8,128)}, f32[136,4096]{1,0:T(8,128)}) custom-call(s32[2176]{0:T(1024)} %select_reduce_fusion.code_ref, bf16[16,32,16,128]{3,2,1,0:T(8,128)(2,1)} %get-tuple-element.78.head_h, bf16[256,16,128]{2,1,0:T(8,128)(2,1)} %bitcast.44, ...), custom_call_target="tpu_custom_call" | custom-call | tf_op jit(solution)/shard_map/pallas_call | solution.py:572
  483.8 0.0 copy-start.2
  483.9 0.0 copy-start.6
  483.9 0.0 copy-start.7
  483.9 0.0 copy-start.1
  483.9 0.0 slice-start
  483.9 2.9 convert_element_type.49
  486.8 1.4 slice.30
  488.2 0.0 slice-start.1
  488.2 2.5 fusion.8
  490.7 0.7 multiply_subtract_fusion.1
  491.4 1.4 copy.41
  492.7 0.0 slice-done
  492.8 2.3 copy.42
  495.0 1.0 copy-done
  496.0 1.4 copy.43
  (27 shorter events, 0.1 us)
Async XLA Ops:
  7.2 95.5 %copy-start.10 = (s32[512]{0:T(512)S(1)}, s32[512]{0:T(512)}, u32[]{:S(2)}) copy-start(s32[512]{0:T(512)} %param.21) | copy-start | bytes 6148
  7.2 95.7 %copy-start.11 = (s32[512]{0:T(512)S(1)}, s32[512]{0:T(512)}, u32[]{:S(2)}) copy-start(s32[512]{0:T(512)} %param.20) | copy-start | bytes 6148
  7.2 95.9 %copy-start.12 = (s32[32]{0:T(128)S(1)}, s32[32]{0:T(128)}, u32[]{:S(2)}) copy-start(s32[32]{0:T(128)} %param.18) | copy-start | bytes 388
  7.2 211.7 %all-gather.3.cloned.1.call-start = ((), (), s32[]{:S(2)}) async-start(), calls=%async_computation | async-start | bytes 4456448 | tf_op jit(solution)/shard_map/all_gather | solution.py:1587
  103.2 6.2 %copy-start.13 = (s32[32]{0:T(128)S(1)}, s32[32]{0:T(128)}, u32[]{:S(2)}) copy-start(s32[32]{0:T(128)} %param.19) | copy-start | bytes 388
  103.2 6.3 %slice-start.2 = ((f32[13288]{0:T(1024)}), f32[1000]{0:T(1024)S(1)}, s32[]{:S(2)}) async-start(f32[13288]{0:T(1024)} %param.29), calls=%async_computation.3 | async-start | bytes 8192 | tf_op jit(solution)/shard_map/slice | solution.py:1603
  103.2 6.9 %copy-start.5 = (f32[13288]{0:T(1024)S(1)}, f32[13288]{0:T(1024)}, u32[]{:S(2)}) copy-start(f32[13288]{0:T(1024)} %param.29) | copy-start | bytes 159460
  164.3 51.4 %copy-start.9 = (s32[2176]{0:T(1024)S(1)}, s32[2176]{0:T(1024)}, u32[]{:S(2)}) copy-start(s32[2176]{0:T(1024)} %param.22) | copy-start | bytes 26116
  164.3 51.3 %copy-start.14 = (s32[2176]{0:T(1024)S(1)}, s32[2176]{0:T(1024)}, u32[]{:S(2)}) copy-start(s32[2176]{0:T(1024)} %constant.102) | copy-start | bytes 26116
  372.9 115.3 %copy-start.8 = (f32[64,128]{1,0:T(8,128)S(1)}, f32[64,128]{1,0:T(8,128)}, u32[]{:S(2)}) copy-start(f32[64,128]{1,0:T(8,128)} %get-tuple-element.98) | copy-start | bytes 98308
  372.9 115.3 %copy-start.3 = (f32[128,1000]{0,1:T(8,128)S(1)}, f32[128,1000]{0,1:T(8,128)}, u32[]{:S(2)}) copy-start(f32[128,1000]{0,1:T(8,128)} %param.28) | copy-start | bytes 1536004
  372.9 115.3 %copy-start.4 = (f32[128,1000]{0,1:T(8,128)S(1)}, f32[128,1000]{0,1:T(8,128)}, u32[]{:S(2)}) copy-start(f32[128,1000]{0,1:T(8,128)} %param.27) | copy-start | bytes 1536004
  483.8 4.3 copy-start.2
  483.9 6.8 %copy-start.6 = (f32[13288]{0:T(1024)S(1)}, f32[13288]{0:T(1024)}, u32[]{:S(2)}) copy-start(f32[13288]{0:T(1024)} %param.31) | copy-start | bytes 159460
  483.9 6.8 %copy-start.7 = (f32[13288]{0:T(1024)S(1)}, f32[13288]{0:T(1024)}, u32[]{:S(2)}) copy-start(f32[13288]{0:T(1024)} %param.30) | copy-start | bytes 159460
  483.9 7.5 %copy-start.1 = (f32[136,4096]{1,0:T(8,128)S(1)}, f32[136,4096]{1,0:T(8,128)}, u32[]{:S(2)}) copy-start(f32[136,4096]{1,0:T(8,128)} %get-tuple-element.127) | copy-start | bytes 6684676
  483.9 8.9 %slice-start = ((s8[4456448]{0:T(1024)(128)(4,1)}), s8[4194304]{0:T(1024)(128)(4,1)S(1)}, s32[]{:S(2)}) async-start(s8[4456448]{0:T(1024)(128)(4,1)} %bitcast.36), calls=%async_computation.1 | async-start | bytes 8388608
  488.2 4.5 slice-start.1
  492.7 3.2 copy-start
Sparse Core Ops, SparseCore 0:
  102.8 77.1 all-gather.2
where the time goes:
time: 514 us; the launch traced here: 505 us
  Pallas kernels  455 us (89%)
  local copies, waits for them, and re-layouts  19 us (4%)
  other arithmetic  16 us (3%)
  between operations  14.7 us (3%)
    pallas_call x2, Pallas kernels, backward_layer(): pl.pallas_call(functools.partial(backward_kernel, devices, top, total_cou...  118 us
    pallas_call x1, Pallas kernels, deliver_blocks(): pl.pallas_call(functools.partial(deliver_kernel, devices, spans), out_sha...  111 us
    pallas_call x2, Pallas kernels, forward_layer(): pl.pallas_call(functools.partial(forward_kernel, devices, top, total_coun...  99.7 us
    pallas_call x1, Pallas kernels, bring_weights(): pl.pallas_call(functools.partial(bring_kernel, devices, spans), out_shape...  92.3 us
    pallas_call x1, Pallas kernels, head_step(): pl.pallas_call(functools.partial(head_kernel, devices, float(HEIGHT * WID...  33.8 us
  transfers between devices with their start and end apart: 1, of which 0 were waited for; matrix products, arithmetic and copies ran while one was open for 3% of the time, Pallas kernels for 20%

commit v1 on v0

--- a/solution.py
+++ b/solution.py
@@ -836,34 +836,34 @@
     return copies
 
 
-def forward_kernel(devices, top, total_count, *refs):
+def forward_kernel(devices, total_count, *refs):
     refs = list(refs)
     take = lambda n: [refs.pop(0) for _ in range(n)]
-    xb_h, xf_h = take(2) if top else [None, None]
-    wi_h, wm_h, wo_h = take(3)
-    if not top:
-        xb, = take(1)
-    params, live = take(2)
-    za_h, hp_h, zb_h, hb_h, zc_h, stat_a, stat_b, stat_c = take(8)
-    if top:
-        pooled, = take(1)
-    else:
-        xn_h, xnb_h = take(2)
-    if top:
-        xb, xf = take(2)
-    wi, wm, wo, za, hp, zb, hb, zc = take(8)
-    if not top:
-        xn, xnb = take(2)
-    stage_m, stage_c, buf_a, buf_b, buf_c = take(5)
+    w_h = [take(3) for _ in range(LAYERS)]
+    x_in, = take(1)
+    params_of = take(LAYERS)
+    live, = take(1)
+    kept_h = [take(5) for _ in range(LAYERS)]
+    stats_of = [take(3) for _ in range(LAYERS)]
+    xn_h, xnb_h, pooled = take(3)
+    wi, wm, wo, za, hp, zb, hb, zc, xn, xnb = take(10)
+    stage_m, stage_c = take(2)
+    bufs_of = [take(3) for _ in range(LAYERS)]
     in_sem, out_sem, send_sem, recv_sem, halo_sem = take(5)
 
     net = Net(devices)
     net.hello()
-    loads = load_all(
-        [(wi_h, wi), (wm_h, wm), (wo_h, wo)] + ([(xb_h, xb), (xf_h, xf)] if top else []), in_sem
-    )
+    loading = {}
+    places = [wi, wm, wo]
+
+    def start(at, which):
+        copy = pltpu.make_async_copy(w_h[at][which], places[which], in_sem.at[at, which])
+        copy.start()
+        loading[at, which] = copy
+
+    for which in range(3):
+        start(0, which)
     clear_edges(hp, net.core)
-    zb[...] = jnp.zeros(zb.shape, F32)
     own_count = jnp.sum(column_sum(live[...]), axis=0, keepdims=True)
     pair_count = total_count / devices
     quarter = za.shape[1] // ROW_SLOTS
@@ -876,136 +876,153 @@
         copy.start()
         stores.append(copy)
 
-    def norm(z, n, stage, bufs, which, masked, stat):
-        local_moments(z, n, live, own_count, stage, masked)
-        if which == 0:
-            net.ready()
-        total, copies = reduce_all(
-            net,
-            stage[...],
-            bufs,
-            send_sem.at[which],
-            recv_sem.at[which],
-            pooled_moments(n),
-            own_count,
-            pair_count,
+    def layer(at):
+        params = params_of[at]
+        stat_a, stat_b, stat_c = stats_of[at]
+        za_h, hp_h, zb_h, hb_h, zc_h = kept_h[at]
+        later = at + 1 < LAYERS
+
+        def norm(z, n, stage, which, masked, stat):
+            local_moments(z, n, live, own_count, stage, masked)
+            if at == 0 and which == 0:
+                net.ready()
+            total, copies = reduce_all(
+                net,
+                stage[...],
+                bufs_of[at][which],
+                send_sem.at[3 * at + which],
+                recv_sem.at[3 * at + which],
+                pooled_moments(n),
+                own_count,
+                pair_count,
+            )
+            sends.extend(copies)
+            stat[0:n] = total[:n] / total_count
+            stat[n : 2 * n] = lax.rsqrt(total[n:] / total_count + EPS_NORM)
+
+        def affine(stat, n, gain_at, j):
+            mean = stat[pl.ds(j, 1)]
+            scale = stat[pl.ds(n + j, 1)] * params[pl.ds(gain_at + j, 1)]
+            return mean, scale, params[pl.ds(gain_at + n + j, 1)]
+
+        loading[at, 0].wait()
+        if at:
+            for copy in stores[:5]:
+                copy.wait()
+        x = lanes_of(xnb, 0, N_IN) if at else x_in[...]
+        product = dot(x, lanes_of(wi, 0, N_MID), 1, 0)
+        for j in range(N_MID):
+            za[j] = product[:, j * LANES : (j + 1) * LANES]
+        if later:
+            start(at + 1, 0)
+        norm(za, N_MID, stage_m, 0, at == 0, stat_a)
+        store(za, za_h)
+
+        def fill_hidden(slot):
+            rows = pl.ds(slot * quarter, quarter)
+
+            def slab(j, carry):
+                mean, scale, shift = affine(stat_a, N_MID, 0, j)
+                y = (za[j, rows] - mean) * scale + shift
+                h = (live[rows] * (y * half_tanh(y))).astype(BF16)
+                hp[j, pl.ds(slot + 1, 1), pl.ds(1, WIDTH)] = h.reshape(1, WIDTH, batch, LANES)
+                return carry
+
+            lax.fori_loop(0, N_MID, slab, 0)
+
+        edge = edge_first(
+            net, fill_hidden, lambda: send_edge(hp, net, halo_sem.at[at, 0], halo_sem.at[at, 1])
         )
-        sends.extend(copies)
-        stat[0:n] = total[:n] / total_count
-        stat[n : 2 * n] = lax.rsqrt(total[n:] / total_count + EPS_NORM)
-
-    def affine(stat, n, gain_at, j):
-        mean = stat[pl.ds(j, 1)]
-        scale = stat[pl.ds(n + j, 1)] * params[pl.ds(gain_at + j, 1)]
-        return mean, scale, params[pl.ds(gain_at + n + j, 1)]
-
-    loads[0].wait()
-    if top:
-        loads[3].wait()
-    product = dot(lanes_of(xb, 0, N_IN) if top else xb[...], lanes_of(wi, 0, N_MID), 1, 0)
-    for j in range(N_MID):
-        za[j] = product[:, j * LANES : (j + 1) * LANES]
-    norm(za, N_MID, stage_m, buf_a, 0, not top, stat_a)
-    store(za, za_h)
-
-    def fill_hidden(slot):
-        rows = pl.ds(slot * quarter, quarter)
-
-        def slab(j, carry):
-            mean, scale, shift = affine(stat_a, N_MID, 0, j)
-            y = (za[j, rows] - mean) * scale + shift
-            h = (live[rows] * (y * half_tanh(y))).astype(BF16)
-            hp[j, pl.ds(slot + 1, 1), pl.ds(1, WIDTH)] = h.reshape(1, WIDTH, batch, LANES)
+        loading[at, 1].wait()
+        zb[...] = jnp.zeros(zb.shape, F32)
+
+        def tap(t):
+            k = pl.ds(pl.multiple_of(t * M, M), M)
+            part = dot(
+                window(hp, t // 3, lax.rem(t, 3)),
+                jnp.concatenate([wm[j, k] for j in range(N_MID)], axis=-1),
+                1,
+                0,
+            )
+            for j in range(N_MID):
+                zb[j] = zb[j] + part[:, j * LANES : (j + 1) * LANES]
+
+        def middle(i, carry):
+            tap(i + 3)
             return carry
 
-        lax.fori_loop(0, N_MID, slab, 0)
-
-    sends.append(
-        edge_first(net, fill_hidden, lambda: send_edge(hp, net, halo_sem.at[0], halo_sem.at[1]))
-    )
-    loads[1].wait()
-
-    def tap(t):
-        k = pl.ds(pl.multiple_of(t * M, M), M)
-        part = dot(
-            window(hp, t // 3, lax.rem(t, 3)),
-            jnp.concatenate([wm[j, k] for j in range(N_MID)], axis=-1),
-            1,
-            0,
-        )
-        for j in range(N_MID):
-            zb[j] = zb[j] + part[:, j * LANES : (j + 1) * LANES]
-
-    def middle(i, carry):
-        tap(i + 3)
-        return carry
-
-    def outer(i, carry):
-        tap(jnp.where(i < 3, i, i + 3))
-        return carry
-
-    lax.fori_loop(0, 3, middle, 0)
-    edge_landed(hp, net, halo_sem.at[1])
-    store(hp, hp_h)
-    lax.fori_loop(0, 6, outer, 0)
-    norm(zb, N_MID, stage_m, buf_b, 1, True, stat_b)
-    store(zb, zb_h)
-
-    def fill_second(j, carry):
-        mean, scale, shift = affine(stat_b, N_MID, 2 * N_MID, j)
-        for q in range(4):
-            rows = pl.ds(q * quarter, quarter)
-            y = (zb[j, rows] - mean) * scale + shift
-            hb[j, rows] = (live[rows] * (y * half_tanh(y))).astype(BF16)
-        return carry
-
-    lax.fori_loop(0, N_MID, fill_second, 0)
-    store(hb, hb_h)
-    loads[2].wait()
-
-    def expand(g, carry):
-        part = dot(lanes_of(hb, 0, N_MID), lanes_of(wo, g * N_MID, N_MID), 1, 0)
-        for j in range(N_MID):
-            zc[g * N_MID + j] = part[:, j * LANES : (j + 1) * LANES]
-        return carry
-
-    lax.fori_loop(0, N_IN // N_MID, expand, 0)
-    store(zc, zc_h)
-    norm(zc, N_IN, stage_c, buf_c, 2, False, stat_c)
-    if top:
-        loads[4].wait()
-
-    def finish(j, carry):
-        mean, scale, shift = affine(stat_c, N_IN, 4 * N_MID, j)
-        pool = jnp.zeros((batch, LANES), F32)
-        for q in range(4):
-            rows = pl.ds(q * quarter, quarter)
-            if top:
-                x = xf[j, rows]
-            else:
-                x = xb[rows, pl.ds(pl.multiple_of(j * LANES, LANES), LANES)].astype(F32)
-            y = (zc[j, rows] - mean) * scale + shift + x
-            out = live[rows] * (y * half_tanh(y))
-            if top:
-                pool = pool + jnp.sum(out.reshape(WIDTH, batch, LANES), axis=0)
-            else:
-                xn[j, rows] = out
-                xnb[j, rows] = out.astype(BF16)
-        if top:
-            pooled[j] = pool
-        return carry
-
-    lax.fori_loop(0, N_IN, finish, 0)
-    if not top:
-        store(xn, xn_h)
-        store(xnb, xnb_h)
-    for copy in stores:
+        def outer(i, carry):
+            tap(jnp.where(i < 3, i, i + 3))
+            return carry
+
+        lax.fori_loop(0, 3, middle, 0)
+        edge_landed(hp, net, halo_sem.at[at, 1])
+        edge.wait_send()
+        store(hp, hp_h)
+        lax.fori_loop(0, 6, outer, 0)
+        if later:
+            start(at + 1, 1)
+        norm(zb, N_MID, stage_m, 1, True, stat_b)
+        store(zb, zb_h)
+
+        def fill_second(j, carry):
+            mean, scale, shift = affine(stat_b, N_MID, 2 * N_MID, j)
+            for q in range(4):
+                rows = pl.ds(q * quarter, quarter)
+                y = (zb[j, rows] - mean) * scale + shift
+                hb[j, rows] = (live[rows] * (y * half_tanh(y))).astype(BF16)
+            return carry
+
+        lax.fori_loop(0, N_MID, fill_second, 0)
+        store(hb, hb_h)
+        loading[at, 2].wait()
+
+        def expand(g, carry):
+            part = dot(lanes_of(hb, 0, N_MID), lanes_of(wo, g * N_MID, N_MID), 1, 0)
+            for j in range(N_MID):
+                zc[g * N_MID + j] = part[:, j * LANES : (j + 1) * LANES]
+            return carry
+
+        lax.fori_loop(0, N_IN // N_MID, expand, 0)
+        if later:
+            start(at + 1, 2)
+        store(zc, zc_h)
+        norm(zc, N_IN, stage_c, 2, False, stat_c)
+
+        def finish(j, carry):
+            mean, scale, shift = affine(stat_c, N_IN, 4 * N_MID, j)
+            pool = jnp.zeros((batch, LANES), F32)
+            for q in range(4):
+                rows = pl.ds(q * quarter, quarter)
+                if at:
+                    x = xn[j, rows]
+                else:
+                    x = x_in[rows, pl.ds(pl.multiple_of(j * LANES, LANES), LANES)].astype(F32)
+                y = (zc[j, rows] - mean) * scale + shift + x
+                out = live[rows] * (y * half_tanh(y))
+                if later:
+                    xn[j, rows] = out
+                    xnb[j, rows] = out.astype(BF16)
+                else:
+                    pool = pool + jnp.sum(out.reshape(WIDTH, batch, LANES), axis=0)
+            if not later:
+                pooled[j] = pool
+            return carry
+
+        lax.fori_loop(0, N_IN, finish, 0)
+        if later:
+            store(xn, xn_h)
+            store(xnb, xnb_h)
+
+    for at in range(LAYERS):
+        layer(at)
+    for copy in stores[5:]:
         copy.wait()
     for copy in sends:
         copy.wait_send()
 
 
-def forward_layer(devices, top, total_count, ident, xb, xf, weights, params, live):
+def forward_pass(devices, total_count, x, weights, params, live):
     rows = live.shape[0]
     batch = rows // ROWS
     shape = jax.ShapeDtypeStruct
@@ -1019,41 +1036,36 @@
         shape((N_IN, rows, LANES), F32),
     ]
     stats = [shape((2 * n, LANES), F32) for n in (N_MID, N_MID, N_IN)]
-    if top:
-        last = [shape((N_IN, batch, LANES), F32)]
-        last_specs = [vmem]
-    else:
-        last = [shape((N_IN, rows, LANES), F32), shape((N_IN, rows, LANES), BF16)]
-        last_specs = [any_space] * 2
+    last = [shape((N_IN, rows, LANES), F32), shape((N_IN, rows, LANES), BF16)]
     big = lambda s: pltpu.VMEM(s.shape, s.dtype)
     total = slots_total(devices)
     dma = pltpu.SemaphoreType.DMA
-    ins = ([xb, xf] if top else []) + list(weights)
-    small_ins = ([] if top else [xb]) + [params, live]
-    return pl.pallas_call(
-        functools.partial(forward_kernel, devices, top, total_count),
-        out_shape=fields + stats + last,
-        in_specs=[any_space] * len(ins) + [vmem] * len(small_ins),
-        out_specs=[any_space] * 5 + [vmem] * 3 + last_specs,
-        scratch_shapes=[big(a) for a in ins]
-        + [big(s) for s in fields]
-        + ([] if top else [big(s) for s in last])
+    small_ins = [x] + list(params) + [live]
+    out = pl.pallas_call(
+        functools.partial(forward_kernel, devices, total_count),
+        out_shape=fields * LAYERS + stats * LAYERS + last + [shape((N_IN, batch, LANES), F32)],
+        in_specs=[any_space] * len(weights) + [vmem] * len(small_ins),
+        out_specs=[any_space] * (5 * LAYERS) + [vmem] * (3 * LAYERS) + [any_space] * 2 + [vmem],
+        scratch_shapes=[big(w) for w in weights[:3]]
+        + [big(s) for s in fields + last]
+        + [pltpu.VMEM((2 * N_MID, LANES), F32), pltpu.VMEM((2 * N_IN, LANES), F32)]
+        + [pltpu.VMEM((total, 2 * n, LANES), F32) for n in (N_MID, N_MID, N_IN)] * LAYERS
         + [
-            pltpu.VMEM((2 * N_MID, LANES), F32),
-            pltpu.VMEM((2 * N_IN, LANES), F32),
-            pltpu.VMEM((total, 2 * N_MID, LANES), F32),
-            pltpu.VMEM((total, 2 * N_MID, LANES), F32),
-            pltpu.VMEM((total, 2 * N_IN, LANES), F32),
-            dma((5,)),
-            dma((8,)),
-            dma((3, total)),
-            dma((3, total)),
-            dma((2,)),
+            dma((LAYERS, 3)),
+            dma((5 * LAYERS + 2,)),
+            dma((3 * LAYERS, total)),
+            dma((3 * LAYERS, total)),
+            dma((LAYERS, 2)),
         ],
         compiler_params=pltpu.CompilerParams(
-            collective_id=ident, has_side_effects=True, vmem_limit_bytes=60 * 2**20
+            collective_id=3, has_side_effects=True, vmem_limit_bytes=60 * 2**20
         ),
-    )(*ins, *small_ins)
+    )(*weights, *small_ins)
+    kept = [
+        list(out[5 * at : 5 * at + 5]) + list(out[5 * LAYERS + 3 * at : 5 * LAYERS + 3 * at + 3])
+        for at in range(LAYERS)
+    ]
+    return kept, out[-3], out[-2], out[-1]
 
 
 def head_kernel(
@@ -1220,65 +1232,59 @@
     return part[:, j * LANES : (j + 1) * LANES].astype(BF16).reshape(-1, 2, HALF, LANES)
 
 
-def backward_kernel(devices, top, total_count, *refs):
+def backward_kernel(devices, total_count, *refs):
     refs = list(refs)
     take = lambda n: [refs.pop(0) for _ in range(n)]
-    field_h = refs.pop(0)
-    xb_h, = take(1) if top else [None]
-    zc_h, hb_h, hp_h, zb_h, za_h, wi_h, wm_h, wo_h = take(8)
-    if not top:
-        xb, = take(1)
-    gtop, stat_a, stat_b, stat_c, params, live, extra = take(7)
-    gi_h, gm_h, go_h = take(3)
-    gout_h, = take(1) if top else [None]
-    small, = take(1)
-    field = refs.pop(0)
-    if top:
-        xb, = take(1)
-    zc, hb, hp, zb, za, wi, wm, wo = take(8)
-    gi, gm, go = take(3)
-    ri, rm, ro = take(3)
-    ec, ep, ea, ub, ua = take(5)
-    stage_m, stage_c, buf_a, buf_b, buf_c = take(5)
+    names = ["zc", "hb", "hp", "zb", "za", "wi", "wm", "wo"]
+    source = {}
+    source["xf", 1], source["xb", 1] = take(2)
+    for at in (0, 1):
+        for name in names:
+            source[name, at] = refs.pop(0)
+    x_in, gtop = take(2)
+    stats_of = [take(3) for _ in range(LAYERS)]
+    params_of = take(LAYERS)
+    live, extra = take(2)
+    out_of = [take(3) for _ in range(LAYERS)]
+    small_of = take(LAYERS)
+    field, xb, zc, hb, hp, zb, za, wi, wm, wo = take(10)
+    place = dict(xf=field, xb=xb, zc=zc, hb=hb, hp=hp, zb=zb, za=za, wi=wi, wm=wm, wo=wo)
+    g_side, g_mid, r_side, r_mid = take(4)
+    ec, ep, ea, ub = take(4)
+    stage_m, stage_c = take(2)
+    bufs_of = [take(3) for _ in range(LAYERS)]
     in_sem, out_sem, send_sem, recv_sem, halo_sem, pair_sem = take(6)
 
     net = Net(devices)
     net.hello()
-    loads = load_all(
-        [
-            (zc_h, zc), (field_h, field), (za_h, za), (wo_h, wo), (zb_h, zb), (hb_h, hb),
-            (hp_h, hp), (wm_h, wm), (wi_h, wi),
-        ]
-        + ([(xb_h, xb)] if top else []),
-        in_sem,
-    )
+    order = ["zc", "xf", "wo", "zb", "hb", "hp", "wm", "za", "wi", "xb"]
+    loading = {}
+
+    def start(name, at):
+        copy = pltpu.make_async_copy(
+            source[name, at], place[name], in_sem.at[at, order.index(name)]
+        )
+        copy.start()
+        loading[name, at] = copy
+
+    def need(name, at):
+        loading[name, at].wait()
+
+    for name in order:
+        start(name, 1)
     clear_edges(ep, net.core)
     quarter = za.shape[1] // ROW_SLOTS
     batch = quarter // WIDTH
-    stores = []
+    groups = N_IN // N_MID
+    side_rows, mid_rows = M // 32, 9 * M // 32
     sends = []
+    stored = []
 
     def store(src, dst):
-        copy = pltpu.make_async_copy(src, dst, out_sem.at[len(stores)])
+        copy = pltpu.make_async_copy(src, dst, out_sem.at[len(stored)])
         copy.start()
-        stores.append(copy)
-
-    def swap(grad, other, at):
-        sends.append(
-            remote(
-                grad.at[:, :, 1 - net.core], other, pair_sem.at[0, at], pair_sem.at[1, at], net.partner
-            )
-        )
-
-    def fold(grad, other, at, out):
-        landed(other, pair_sem.at[1, at])
-
-        def step(i, carry):
-            other[:, i] = (grad[:, i, net.core].astype(F32) + other[:, i].astype(F32)).astype(BF16)
-            return carry
-
-        lax.fori_loop(0, grad.shape[1], step, 0)
-        store(other, out)
+        stored.append(copy)
+        return copy
 
     def slope(y):
         sigma = half_tanh(y)
@@ -1287,261 +1293,325 @@
     def row(ref, j):
         return ref[pl.ds(j, 1)]
 
-    def totals(stage, bufs, which, small_at, n, fillers=()):
-        total, copies = reduce_all(
-            net, stage[...], bufs, send_sem.at[which], recv_sem.at[which], plain_sum, fillers=fillers
+    def swap(grad, other, at, which):
+        return remote(
+            grad.at[:, 1 - net.core],
+            other,
+            pair_sem.at[at, 0, which],
+            pair_sem.at[at, 1, which],
+            net.partner,
         )
-        sends.extend(copies)
-        small[small_at : small_at + 2 * n] = total[: 2 * n]
-        return total
-
-    loads[0].wait()
-    loads[1].wait()
-
-    def slab_c(j, carry):
-        mean, scale = row(stat_c, j), row(stat_c, N_IN + j)
-        gain, shift = row(params, 4 * N_MID + j), row(params, 4 * N_MID + N_IN + j)
-        total = jnp.zeros((8, LANES), F32)
-        crossed = jnp.zeros((8, LANES), F32)
-        for q in range(4):
-            rows = pl.ds(q * quarter, quarter)
-            normed = (zc[j, rows] - mean) * scale
+
+    def fold(copy, grad, other, at, which, out):
+        landed(other, pair_sem.at[at, 1, which])
+        copy.wait_send()
+
+        def step(i, carry):
+            part = pl.ds(i * 16, 16)
+            other[part] = (grad[part, net.core].astype(F32) + other[part].astype(F32)).astype(BF16)
+            return carry
+
+        lax.fori_loop(0, grad.shape[0] // 16, step, 0)
+        return store(other, out)
+
+    def layer(at, fillers):
+        top = at == 1
+        stat_a, stat_b, stat_c = stats_of[at]
+        params, small = params_of[at], small_of[at]
+        gi_h, gm_h, go_h = out_of[at]
+        state = {}
+
+        def refill(name):
             if top:
-                x = field[j, rows]
-                g = jnp.concatenate([gtop[j]] * WIDTH, axis=0)
-            else:
-                x = xb[rows, pl.ds(pl.multiple_of(j * LANES, LANES), LANES)].astype(F32)
-                g = field[j, rows]
-            u = g * live[rows] * slope(normed * gain + shift + x)
-            field[j, rows] = u
-            total = total + column_sum(u)
-            crossed = crossed + column_sum(u * normed)
-        stage_c[pl.ds(j, 1)] = jnp.sum(crossed, axis=0, keepdims=True)
-        stage_c[pl.ds(N_IN + j, 1)] = jnp.sum(total, axis=0, keepdims=True)
-        return carry
-
-    lax.fori_loop(0, N_IN, slab_c, 0)
-    stage_c[2 * N_IN :] = extra[...]
-    net.ready()
-    total_c = totals(stage_c, buf_c, 2, 4 * N_MID, N_IN)
-    small[4 * N_MID + 2 * N_IN :] = total_c[2 * N_IN :]
-
-    def back_c(j, carry):
-        mean, scale = row(stat_c, j), row(stat_c, N_IN + j)
-        gain = row(params, 4 * N_MID + j)
-        cross = row(small, 4 * N_MID + j) / total_count
-        plain = row(small, 4 * N_MID + N_IN + j) / total_count
-        for q in range(4):
-            rows = pl.ds(q * quarter, quarter)
-            normed = (zc[j, rows] - mean) * scale
-            e = live[rows] * ((gain * scale) * (field[j, rows] - plain - normed * cross))
-            ec[j, rows] = e.astype(BF16)
-        return carry
-
-    lax.fori_loop(0, N_IN, back_c, 0)
-    loads[3].wait()
-    product = dot(lanes_of(ec, 0, N_IN), lanes_of(wo, 0, N_IN), 1, 1)
-    for j in range(N_MID):
-        ub[j] = product[:, j * LANES : (j + 1) * LANES]
-    loads[4].wait()
-
-    def sums_of(u_ref, z_ref, stat, gain_at, stage):
-        def slab(j, carry):
-            mean, scale = row(stat, j), row(stat, N_MID + j)
-            gain, shift = row(params, gain_at + j), row(params, gain_at + N_MID + j)
+                start(name, 0)
+
+        def totals(stage, which, small_at, n, fillers):
+            total, copies = reduce_all(
+                net,
+                stage[...],
+                bufs_of[at][which],
+                send_sem.at[3 * at + which],
+                recv_sem.at[3 * at + which],
+                plain_sum,
+                fillers=fillers,
+            )
+            sends.extend(copies)
+            small[small_at : small_at + 2 * n] = total[: 2 * n]
+            return total
+
+        need("zc", at)
+        if top:
+            need("xf", at)
+
+        def slab_c(j, carry):
+            mean, scale = row(stat_c, j), row(stat_c, N_IN + j)
+            gain, shift = row(params, 4 * N_MID + j), row(params, 4 * N_MID + N_IN + j)
             total = jnp.zeros((8, LANES), F32)
             crossed = jnp.zeros((8, LANES), F32)
             for q in range(4):
                 rows = pl.ds(q * quarter, quarter)
-                normed = (z_ref[j, rows] - mean) * scale
-                u = u_ref[j, rows] * live[rows] * slope(normed * gain + shift)
-                u_ref[j, rows] = u
+                normed = (zc[j, rows] - mean) * scale
+                if top:
+                    x = field[j, rows]
+                    g = jnp.concatenate([gtop[j]] * WIDTH, axis=0)
+                else:
+                    x = x_in[rows, pl.ds(pl.multiple_of(j * LANES, LANES), LANES)].astype(F32)
+                    g = field[j, rows]
+                u = g * live[rows] * slope(normed * gain + shift + x)
+                field[j, rows] = u
                 total = total + column_sum(u)
                 crossed = crossed + column_sum(u * normed)
-            stage[pl.ds(j, 1)] = jnp.sum(crossed, axis=0, keepdims=True)
-            stage[pl.ds(N_MID + j, 1)] = jnp.sum(total, axis=0, keepdims=True)
+            stage_c[pl.ds(j, 1)] = jnp.sum(crossed, axis=0, keepdims=True)
+            stage_c[pl.ds(N_IN + j, 1)] = jnp.sum(total, axis=0, keepdims=True)
             return carry
 
-        lax.fori_loop(0, N_MID, slab, 0)
-
-    def back_of(u_ref, z_ref, stat, gain_at, small_at, j, rows):
-        normed = (z_ref[j, rows] - row(stat, j)) * row(stat, N_MID + j)
-        cross = row(small, small_at + j) / total_count
-        plain = row(small, small_at + N_MID + j) / total_count
-        factor = row(params, gain_at + j) * row(stat, N_MID + j)
-        return (live[rows] * (factor * (u_ref[j, rows] - plain - normed * cross))).astype(BF16)
-
-    sums_of(ub, zb, stat_b, 2 * N_MID, stage_m)
-    loads[5].wait()
-
-    def grad_out(first, last):
-        def group(g, carry):
-            part = dot(lanes_of(hb, 0, N_MID), lanes_of(ec, g * N_MID, N_MID), 0, 0)
-            for j in range(N_MID):
-                go[g * N_MID + j] = pieces(part, j)
+        lax.fori_loop(0, N_IN, slab_c, 0)
+        if top:
+            stage_c[2 * N_IN :] = extra[...]
+            net.ready()
+        else:
+            stage_c[2 * N_IN :] = jnp.zeros(extra.shape, F32)
+        total_c = totals(stage_c, 2, 4 * N_MID, N_IN, fillers)
+        small[4 * N_MID + 2 * N_IN :] = total_c[2 * N_IN :]
+
+        def back_c(j, carry):
+            mean, scale = row(stat_c, j), row(stat_c, N_IN + j)
+            gain = row(params, 4 * N_MID + j)
+            cross = row(small, 4 * N_MID + j) / total_count
+            plain = row(small, 4 * N_MID + N_IN + j) / total_count
+            for q in range(4):
+                rows = pl.ds(q * quarter, quarter)
+                normed = (zc[j, rows] - mean) * scale
+                e = live[rows] * ((gain * scale) * (field[j, rows] - plain - normed * cross))
+                ec[j, rows] = e.astype(BF16)
             return carry
 
-        return lambda: lax.fori_loop(first, last, group, 0)
-
-    groups = N_IN // N_MID
-    totals(
-        stage_m, buf_b, 1, 2 * N_MID, N_MID,
-        [grad_out(0, 1), grad_out(1, groups - 1), grad_out(groups - 1, groups)],
-    )
-    swap(go, ro, 0)
-
-    def fill_b(slot):
-        rows = pl.ds(slot * quarter, quarter)
-
-        def slab(j, carry):
-            e = back_of(ub, zb, stat_b, 2 * N_MID, 2 * N_MID, j, rows)
-            ep[j, pl.ds(slot + 1, 1), pl.ds(1, WIDTH)] = e.reshape(1, WIDTH, batch, LANES)
-            return carry
-
-        lax.fori_loop(0, N_MID, slab, 0)
-
-    sends.append(
-        edge_first(net, fill_b, lambda: send_edge(ep, net, halo_sem.at[0], halo_sem.at[1]))
-    )
-    loads[6].wait()
-    loads[7].wait()
-    ua[...] = jnp.zeros(ua.shape, F32)
-
-    def grad_mid(first, last):
-        def one(t, carry):
-            part = dot(window(hp, t // 3, lax.rem(t, 3)), window(ep, 1, 1), 0, 0)
-            for j in range(N_MID):
-                gm[j, pl.ds(t * (M // 32), M // 32)] = pieces(part, j)
-            return carry
-
-        return lambda: lax.fori_loop(first, last, one, 0)
-
-    def tap(t):
-        k = pl.ds(pl.multiple_of(t * M, M), M)
-        part = dot(
-            window(ep, 2 - t // 3, 2 - lax.rem(t, 3)),
-            jnp.concatenate([wm[j, k] for j in range(N_MID)], axis=-1),
-            1,
-            1,
+        lax.fori_loop(0, N_IN, back_c, 0)
+        refill("zc")
+        need("wo", at)
+        product = dot(lanes_of(ec, 0, N_IN), lanes_of(wo, 0, N_IN), 1, 1)
+        for j in range(N_MID):
+            ub[j] = product[:, j * LANES : (j + 1) * LANES]
+        refill("wo")
+        need("zb", at)
+
+        def sums_of(z_ref, stat, gain_at):
+            def slab(j, carry):
+                mean, scale = row(stat, j), row(stat, N_MID + j)
+                gain, shift = row(params, gain_at + j), row(params, gain_at + N_MID + j)
+                total = jnp.zeros((8, LANES), F32)
+                crossed = jnp.zeros((8, LANES), F32)
+                for q in range(4):
+                    rows = pl.ds(q * quarter, quarter)
+                    normed = (z_ref[j, rows] - mean) * scale
+                    u = ub[j, rows] * live[rows] * slope(normed * gain + shift)
+                    ub[j, rows] = u
+                    total = total + column_sum(u)
+                    crossed = crossed + column_sum(u * normed)
+                stage_m[pl.ds(j, 1)] = jnp.sum(crossed, axis=0, keepdims=True)
+                stage_m[pl.ds(N_MID + j, 1)] = jnp.sum(total, axis=0, keepdims=True)
+                return carry
+
+            lax.fori_loop(0, N_MID, slab, 0)
+
+        def back_of(z_ref, stat, gain_at, j, rows):
+            normed = (z_ref[j, rows] - row(stat, j)) * row(stat, N_MID + j)
+            cross = row(small, gain_at + j) / total_count
+            plain = row(small, gain_at + N_MID + j) / total_count
+            factor = row(params, gain_at + j) * row(stat, N_MID + j)
+            return (live[rows] * (factor * (ub[j, rows] - plain - normed * cross))).astype(BF16)
+
+        sums_of(zb, stat_b, 2 * N_MID)
+        need("hb", at)
+
+        def grad_out(first, last):
+            def group(g, carry):
+                part = dot(lanes_of(hb, 0, N_MID), lanes_of(ec, g * N_MID, N_MID), 0, 0)
+                for j in range(N_MID):
+                    g_side[pl.ds((g * N_MID + j) * side_rows, side_rows)] = pieces(part, j)
+                return carry
+
+            return lambda: lax.fori_loop(first, last, group, 0)
+
+        totals(
+            stage_m, 1, 2 * N_MID, N_MID,
+            [grad_out(0, 1), grad_out(1, groups - 1), grad_out(groups - 1, groups)],
         )
-        for j in range(N_MID):
-            ua[j] = ua[j] + part[:, j * LANES : (j + 1) * LANES]
-
-    def middle(i, carry):
-        tap(i + 3)
-        return carry
-
-    def outer(i, carry):
-        tap(jnp.where(i < 3, i, i + 3))
-        return carry
-
-    lax.fori_loop(0, 3, middle, 0)
-    edge_landed(ep, net, halo_sem.at[1])
-    lax.fori_loop(0, 6, outer, 0)
-    fold(go, ro, 0, go_h)
-    loads[2].wait()
-    sums_of(ua, za, stat_a, 0, stage_m)
-    totals(
-        stage_m, buf_a, 0, 0, N_MID, [grad_mid(0, 2), grad_mid(2, 5), grad_mid(5, 9)]
-    )
-    swap(gm, rm, 1)
-
-    def fill_a(j, carry):
-        for q in range(4):
-            rows = pl.ds(q * quarter, quarter)
-            ea[j, rows] = back_of(ua, za, stat_a, 0, 0, j, rows)
-        return carry
-
-    lax.fori_loop(0, N_MID, fill_a, 0)
-    if top:
-        loads[9].wait()
-
-    def grad_in(g, carry):
-        if top:
-            x = lanes_of(xb, g * N_MID, N_MID)
-        else:
-            x = xb[:, pl.ds(pl.multiple_of(g * M, M), M)]
-        part = dot(x, lanes_of(ea, 0, N_MID), 0, 0)
-        for j in range(N_MID):
-            gi[j, pl.ds(g * (M // 32), M // 32)] = pieces(part, j)
-        return carry
-
-    lax.fori_loop(0, groups, grad_in, 0)
-    swap(gi, ri, 2)
-    loads[8].wait()
-    if top:
-
-        def grad_field(g, carry):
-            k = pl.ds(pl.multiple_of(g * M, M), M)
+        refill("hb")
+        out_swap = swap(g_side, r_side, at, 0)
+
+        def fill_b(slot):
+            rows = pl.ds(slot * quarter, quarter)
+
+            def slab(j, carry):
+                e = back_of(zb, stat_b, 2 * N_MID, j, rows)
+                ep[j, pl.ds(slot + 1, 1), pl.ds(1, WIDTH)] = e.reshape(1, WIDTH, batch, LANES)
+                return carry
+
+            lax.fori_loop(0, N_MID, slab, 0)
+
+        edge = edge_first(
+            net, fill_b, lambda: send_edge(ep, net, halo_sem.at[at, 0], halo_sem.at[at, 1])
+        )
+        refill("zb")
+        need("hp", at)
+        need("wm", at)
+        ub[...] = jnp.zeros(ub.shape, F32)
+
+        def grad_mid(first, last):
+            def one(t, carry):
+                part = dot(window(hp, t // 3, lax.rem(t, 3)), window(ep, 1, 1), 0, 0)
+                for j in range(N_MID):
+                    g_mid[pl.ds(j * mid_rows + t * side_rows, side_rows)] = pieces(part, j)
+                return carry
+
+            return lambda: lax.fori_loop(first, last, one, 0)
+
+        def tap(t):
+            k = pl.ds(pl.multiple_of(t * M, M), M)
             part = dot(
-                lanes_of(ea, 0, N_MID),
-                jnp.concatenate([wi[j, k] for j in range(N_MID)], axis=-1),
+                window(ep, 2 - t // 3, 2 - lax.rem(t, 3)),
+                jnp.concatenate([wm[j, k] for j in range(N_MID)], axis=-1),
                 1,
                 1,
             )
             for j in range(N_MID):
-                at = g * N_MID + j
-                field[at] = field[at] + part[:, j * LANES : (j + 1) * LANES]
+                ub[j] = ub[j] + part[:, j * LANES : (j + 1) * LANES]
+
+        def middle(i, carry):
+            tap(i + 3)
             return carry
 
-        lax.fori_loop(0, groups, grad_field, 0)
-        store(field, gout_h)
-    fold(gm, rm, 1, gm_h)
-    fold(gi, ri, 2, gi_h)
-    for copy in stores:
-        copy.wait()
+        def outer(i, carry):
+            tap(jnp.where(i < 3, i, i + 3))
+            return carry
+
+        lax.fori_loop(0, 3, middle, 0)
+        edge_landed(ep, net, halo_sem.at[at, 1])
+        edge.wait_send()
+        lax.fori_loop(0, 6, outer, 0)
+        refill("wm")
+        out_store = fold(out_swap, g_side, r_side, at, 0, go_h)
+        need("za", at)
+        sums_of(za, stat_a, 0)
+        out_store.wait()
+        totals(stage_m, 0, 0, N_MID, [grad_mid(0, 2), grad_mid(2, 5), grad_mid(5, 9)])
+        refill("hp")
+        mid_swap = swap(g_mid, r_mid, at, 1)
+
+        def fill_a(j, carry):
+            for q in range(4):
+                rows = pl.ds(q * quarter, quarter)
+                ea[j, rows] = back_of(za, stat_a, 0, j, rows)
+            return carry
+
+        lax.fori_loop(0, N_MID, fill_a, 0)
+        refill("za")
+        if top:
+            need("wi", at)
+
+            def grad_field(g, carry):
+                k = pl.ds(pl.multiple_of(g * M, M), M)
+                part = dot(
+                    lanes_of(ea, 0, N_MID),
+                    jnp.concatenate([wi[j, k] for j in range(N_MID)], axis=-1),
+                    1,
+                    1,
+                )
+                for j in range(N_MID):
+                    slab = g * N_MID + j
+                    field[slab] = field[slab] + part[:, j * LANES : (j + 1) * LANES]
+                return carry
+
+            lax.fori_loop(0, groups, grad_field, 0)
+
+        def grad_in(g, carry):
+            if top:
+                x = lanes_of(xb, g * N_MID, N_MID)
+            else:
+                x = x_in[:, pl.ds(pl.multiple_of(g * M, M), M)]
+            part = dot(x, lanes_of(ea, 0, N_MID), 0, 0)
+            for j in range(N_MID):
+                g_side[pl.ds((j * groups + g) * side_rows, side_rows)] = pieces(part, j)
+            return carry
+
+        def first_part():
+            if top:
+                need("xb", at)
+            lax.fori_loop(0, groups, grad_in, 0)
+            state["swap"] = swap(g_side, r_side, at, 2)
+
+        def second_part():
+            state["mid"] = fold(mid_swap, g_mid, r_mid, at, 1, gm_h)
+
+        def third_part():
+            state["in"] = fold(state["swap"], g_side, r_side, at, 2, gi_h)
+            state["mid"].wait()
+            state["in"].wait()
+
+        return [first_part, second_part, third_part]
+
+    rest = layer(1, [])
+    for step in layer(0, rest):
+        step()
     for copy in sends:
         copy.wait_send()
 
 
-def backward_layer(
-    devices, top, total_count, ident, field, xb, kept, weights, gtop, params, live, extra
-):
-    za, hp, zb, hb, zc, stat_a, stat_b, stat_c = kept
-    wi, wm, wo = weights
+def backward_pass(devices, total_count, xf, xb, kept, weights, x, gtop, params, live, extra):
     shape = jax.ShapeDtypeStruct
     any_space = pl.BlockSpec(memory_space=pl.ANY)
     vmem = pl.BlockSpec(memory_space=pltpu.VMEM)
     dma = pltpu.SemaphoreType.DMA
     total = slots_total(devices)
-    rows = za.shape[1]
+    rows = live.shape[0]
     big = lambda s: pltpu.VMEM(s.shape, s.dtype)
-    ins = [field] + ([xb] if top else []) + [zc, hb, hp, zb, za, wi, wm, wo]
-    small_ins = ([] if top else [xb]) + [gtop, stat_a, stat_b, stat_c, params, live, extra]
-    grads = [shape((w.shape[0], w.shape[1] // 32, HALF, LANES), BF16) for w in weights]
-    both = [shape((w.shape[0], w.shape[1] // 32, 2, HALF, LANES), BF16) for w in weights]
-    more = [shape(field.shape, F32)] if top else []
+    each = []
+    for at in range(LAYERS):
+        za, hp, zb, hb, zc = kept[at][:5]
+        each.append([zc, hb, hp, zb, za] + list(weights[3 * at : 3 * at + 3]))
+    ins = [xf, xb] + each[0] + each[1]
+    small_ins = [x, gtop]
+    for at in range(LAYERS):
+        small_ins += kept[at][5:]
+    small_ins += list(params) + [live, extra]
+    side = N_IN * M // 32
+    middle = N_MID * 9 * M // 32
     small_rows = 4 * N_MID + 2 * N_IN + extra.shape[0]
-    return pl.pallas_call(
-        functools.partial(backward_kernel, devices, top, total_count),
-        out_shape=grads + more + [shape((small_rows, LANES), F32)],
+    stage_rows = [2 * N_MID, 2 * N_MID, 2 * N_IN + extra.shape[0]]
+    grads = [shape((n, HALF, LANES), BF16) for n in (side, middle, side)]
+    out = pl.pallas_call(
+        functools.partial(backward_kernel, devices, total_count),
+        out_shape=grads * LAYERS + [shape((small_rows, LANES), F32)] * LAYERS,
         in_specs=[any_space] * len(ins) + [vmem] * len(small_ins),
-        out_specs=[any_space] * (3 + len(more)) + [vmem],
-        scratch_shapes=[big(a) for a in ins]
-        + [big(g) for g in both]
-        + [big(g) for g in grads]
+        out_specs=[any_space] * (3 * LAYERS) + [vmem] * LAYERS,
+        scratch_shapes=[big(a) for a in [xf, xb] + each[0]]
         + [
+            pltpu.VMEM((side, 2, HALF, LANES), BF16),
+            pltpu.VMEM((middle, 2, HALF, LANES), BF16),
+            pltpu.VMEM((side, HALF, LANES), BF16),
+            pltpu.VMEM((middle, HALF, LANES), BF16),
             pltpu.VMEM((N_IN, rows, LANES), BF16),
-            pltpu.VMEM(hp.shape, BF16),
+            pltpu.VMEM(kept[0][1].shape, BF16),
             pltpu.VMEM((N_MID, rows, LANES), BF16),
             pltpu.VMEM((N_MID, rows, LANES), F32),
-            pltpu.VMEM((N_MID, rows, LANES), F32),
             pltpu.VMEM((2 * N_MID, LANES), F32),
-            pltpu.VMEM((2 * N_IN + extra.shape[0], LANES), F32),
-            pltpu.VMEM((total, 2 * N_MID, LANES), F32),
-            pltpu.VMEM((total, 2 * N_MID, LANES), F32),
-            pltpu.VMEM((total, 2 * N_IN + extra.shape[0], LANES), F32),
-            dma((10,)),
-            dma((4,)),
-            dma((3, total)),
-            dma((3, total)),
-            dma((2,)),
-            dma((2, 3)),
+            pltpu.VMEM((stage_rows[2], LANES), F32),
+        ]
+        + [pltpu.VMEM((total, n, LANES), F32) for n in stage_rows] * LAYERS
+        + [
+            dma((LAYERS, 10)),
+            dma((3 * LAYERS,)),
+            dma((3 * LAYERS, total)),
+            dma((3 * LAYERS, total)),
+            dma((LAYERS, 2)),
+            dma((LAYERS, 2, 3)),
         ],
         compiler_params=pltpu.CompilerParams(
-            collective_id=ident, has_side_effects=True, vmem_limit_bytes=62 * 2**20
+            collective_id=6, has_side_effects=True, vmem_limit_bytes=62 * 2**20
         ),
     )(*ins, *small_ins)
+    return out[: 3 * LAYERS], out[3 * LAYERS :]
 
 
 def adamw(values_old, gradient, moment_one, moment_two, step_rate):
@@ -1602,28 +1672,9 @@
     ]
     bias = jnp.pad(small_params[LAYERS * stride :], (0, WIDE - CLASSES))[None, :]
 
-    kept = []
-    field, low = None, first
-    lows = []
-    for at in range(LAYERS):
-        last = at == LAYERS - 1
-        lows.append(low)
-        out = forward_layer(
-            devices,
-            at > 0,
-            live_count,
-            3 + at,
-            low,
-            field,
-            weights[3 * at : 3 * at + 3],
-            params[at],
-            live_rows,
-        )
-        kept.append(out[:8])
-        if last:
-            pooled = out[8]
-        else:
-            field, low = out[8], out[9]
+    kept, field, low, pooled = forward_pass(
+        devices, live_count, first, weights, params, live_rows
+    )
 
     def by_core(v):
         return v.reshape(devices, 2, half_batch).transpose(1, 0, 2).reshape(-1)
@@ -1663,18 +1714,11 @@
             .transpose(1, 0, 2)
             .reshape(devices, head_blocks, HALF, LANES)
         )
-    no_extra = jnp.zeros_like(extra)
-    top = backward_layer(
-        devices, True, live_count, 6, field, lows[1], kept[1], weights[3:], g_top, params[1],
-        live_rows, extra,
-    )
-    bottom = backward_layer(
-        devices, False, live_count, 7, top[3], lows[0], kept[0], weights[:3], no_extra, params[0],
-        live_rows, no_extra,
-    )
-    small_top, small_bottom = top[4], bottom[3]
+    grads, (small_bottom, small_top) = backward_pass(
+        devices, live_count, field, low, kept, weights, first, g_top, params, live_rows, extra
+    )
     head_sum, conv_grad, stats_new, master_new = deliver_blocks(
-        list(bottom[:3]) + list(top[:3]),
+        grads,
         grad_head,
         block_places(owner_slot),
         conv_master,

time: 514 us -> 492 us (0.957)
  Pallas kernels: 455 us -> 434 us
    pallas_call x4 -> x2, Pallas kernels: 218 us -> 197 us  [the longest x1 107 us: backward_pass(): pl.pallas_call(functools.partial(backward_kernel, devices, total_count),...]
  transfers between devices with their start and end apart: 1 -> 1, of which waited for: 0 -> 0; matrix products, arithmetic and copies ran while one was open for 3% -> 3% of each run, Pallas kernels for 20% -> 19%
where the time goes in v1:
time: 492 us; the launch traced here: 483 us
  Pallas kernels  434 us (88%)
  local copies, waits for them, and re-layouts  18.4 us (4%)
  other arithmetic  16 us (3%)
  between operations  14.5 us (3%)
    pallas_call x1, Pallas kernels, deliver_blocks(): pl.pallas_call(functools.partial(deliver_kernel, devices, spans), out_sha...  110 us
    pallas_call x1, Pallas kernels, backward_pass(): pl.pallas_call(functools.partial(backward_kernel, devices, total_count),...  107 us
    pallas_call x1, Pallas kernels, bring_weights(): pl.pallas_call(functools.partial(bring_kernel, devices, spans), out_shape...  92.2 us
    pallas_call x1, Pallas kernels, forward_pass(): pl.pallas_call(functools.partial(forward_kernel, devices, total_count), o...  89.9 us
    pallas_call x1, Pallas kernels, head_step(): pl.pallas_call(functools.partial(head_kernel, devices, float(HEIGHT * WID...  34.5 us
  transfers between devices with their start and end apart: 1, of which 0 were waited for; matrix products, arithmetic and copies ran while one was open for 3% of the time, Pallas kernels for 19%

profile of v1, /device:TPU:0, one launch (start us, length us, event | category | flops | bytes accessed | tf_op | source)
XLA Modules:
  0.0 483.0 jit_solution(2823880245676186521)
XLA Ops:
  7.2 0.0 copy-start.10
  7.2 0.0 copy-start.11
  7.2 0.0 copy-start.12
  7.2 0.0 all-gather.3.cloned.1.call-start
  7.3 1.3 fusion.5.idx_ref
  8.6 1.1 convert_bitcast_fusion
  9.6 92.2 %shard_map.264 = (bf16[4,2048,128]{2,1,0:T(8,128)(2,1)}, bf16[4,4608,128]{2,1,0:T(8,128)(2,1)}, bf16[16,512,128]{2,1,0:T(8,128)(2,1)}, bf16[4,2048,128]{2,1,0:T(...) custom-call(s32[2176]{0:T(1024)} %fusion.5.idx_ref, f32[136,4096]{1,0:T(8,128)} %refs_6_.1), custom_call_target="tpu_custom_call" | custom-call | tf_op jit(solution)/shard_map/pallas_call | solution.py:262
  101.8 0.7 pad.8
  102.5 0.0 all-gather.3.cloned.1.call-update
  102.6 0.0 copy-done.10
  102.6 0.1 reshape.191
  102.7 0.1 dynamic_slice.10
  102.8 0.0 copy-done.11
  102.8 0.1 reshape.190
  102.9 0.1 dynamic_slice.9
  102.9 0.0 copy-done.12
  103.0 0.1 and_convert_fusion
  103.0 0.1 broadcast_in_dim.75
  103.1 5.9 %copy.35 = bf16[4,7,32,2048]{3,2,1,0:T(8,128)(2,1)} copy(bf16[4,7,32,2048]{3,0,1,2:T(4,128)(2,1)} %bitcast.33) | data formatting | bytes 7340032 | tf_op jit(solution)/shard_map/transpose | solution.py:1668
  109.0 0.1 mul.111
  109.1 0.1 eq.83
  109.2 0.1 reshape.189
  109.3 0.0 copy-done.13
  109.3 0.1 dynamic_slice.11
  109.4 0.0 slice-done.2
  109.4 0.6 pad.9
  110.0 0.0 copy-done.5
  110.0 0.6 slice_bitcast_fusion.2
  110.6 1.0 broadcast_in_dim.76.refs_9_.refs_28_
  111.6 89.9 %shard_map.265 = (f32[4,896,128]{2,1,0:T(8,128)}, bf16[4,6,9,32,128]{4,3,2,1,0:T(8,128)(2,1)}, f32[4,896,128]{2,1,0:T(8,128)}, bf16[4,896,128]{2,1,0:T(8,128)(2,...) custom-call(bf16[4,2048,128]{2,1,0:T(8,128)(2,1)} %get-tuple-element, ...), custom_call_target="tpu_custom_call" | custom-call | tf_op jit(solution)/shard_map/pallas_call | solution.py:1044
  201.5 0.6 convert_reduce_fusion
  202.1 0.2 select_reduce_fusion.1
  202.3 1.3 select_select_fusion.numbers
  203.6 0.7 compare_convert_fusion.pick
  204.3 0.7 select_convert_fusion.point
  205.0 0.7 fusion.2.hot
  205.7 0.0 copy-done.9
  205.7 0.0 copy-done.14
  205.7 3.3 select_reduce_fusion.code_ref
  209.0 34.5 %shard_map.266 = (f32[16,128]{1,0:T(8,128)}, f32[16,32,128]{2,1,0:T(8,128)}, bf16[16,32,16,128]{3,2,1,0:T(8,128)(2,1)}) custom-call(f32[16,32,128]{2,1,0:T(8,128)} %get-tuple-element.74.pooled, bf16[16,1024,128]{2,1,0:T(8,128)(2,1)} %bitcast.32, f32[1,1024]{1,0:T(1,128)} %bitcast.38, bf16[16,512]{1,0:T(8,128)(2,1)} %compare_convert_fusion.pick, ...), custom_call_target="tpu_custom_call" | custom-call | tf_op jit(solution)/shard_map/pallas_call | solution.py:1199
  243.5 107.0 %shard_map.267 = (bf16[256,16,128]{2,1,0:T(8,128)(2,1)}, bf16[576,16,128]{2,1,0:T(8,128)(2,1)}, bf16[256,16,128]{2,1,0:T(8,128)(2,1)}, bf16[256,16,128]{2,1,0:T(...) custom-call(f32[16,896,128]{2,1,0:T(8,128)} %get-tuple-element.62.re, ...), custom_call_target="tpu_custom_call" | custom-call | tf_op jit(solution)/shard_map/pallas_call | solution.py:1583
  350.5 0.7 slice_bitcast_fusion
  351.3 0.7 slice_bitcast_fusion.4
  351.9 110.4 %shard_map.268 = (bf16[2,32,16,128]{3,2,1,0:T(8,128)(2,1)}, f32[136,4096]{1,0:T(8,128)}, f32[136,64,128]{2,1,0:T(8,128)}, f32[136,4096]{1,0:T(8,128)}) custom-call(s32[2176]{0:T(1024)} %select_reduce_fusion.code_ref, bf16[16,32,16,128]{3,2,1,0:T(8,128)(2,1)} %get-tuple-element.85.head_h, bf16[256,16,128]{2,1,0:T(8,128)(2,1)} %get-tuple-element.86.refs_0_, ...), custom_call_target="tpu_custom_call" | custom-call | tf_op jit(solution)/shard_map/pallas_call | solution.py:572
  462.4 0.0 copy-start.2
  462.4 0.0 copy-start.6
  462.4 0.0 copy-start.7
  462.4 0.0 copy-start.1
  462.4 0.0 slice-start
  462.4 2.9 convert_element_type.49
  465.4 1.4 slice.30
  466.7 0.0 copy-done.8
  466.7 0.0 copy-done.3
  466.7 0.0 copy-done.4
  466.7 0.0 copy-done.2
  466.7 0.0 slice-start.1
  466.7 2.5 fusion.8
  469.2 0.0 copy-done.6
  469.2 0.0 copy-done.7
  469.2 0.7 multiply_subtract_fusion.1
  469.9 1.4 copy.41
  471.3 2.3 copy.42
  473.6 1.0 copy-done
  474.5 1.4 copy.43
  (24 shorter events, 0.1 us)
Async XLA Ops:
  7.2 95.4 %copy-start.10 = (s32[512]{0:T(512)S(1)}, s32[512]{0:T(512)}, u32[]{:S(2)}) copy-start(s32[512]{0:T(512)} %param.21) | copy-start | bytes 6148
  7.2 95.6 %copy-start.11 = (s32[512]{0:T(512)S(1)}, s32[512]{0:T(512)}, u32[]{:S(2)}) copy-start(s32[512]{0:T(512)} %param.20) | copy-start | bytes 6148
  7.2 95.7 %copy-start.12 = (s32[32]{0:T(128)S(1)}, s32[32]{0:T(128)}, u32[]{:S(2)}) copy-start(s32[32]{0:T(128)} %param.18) | copy-start | bytes 388
  7.2 201.8 %all-gather.3.cloned.1.call-start = ((), (), s32[]{:S(2)}) async-start(), calls=%async_computation | async-start | bytes 4456448 | tf_op jit(solution)/shard_map/all_gather | solution.py:1657
  103.1 6.2 %copy-start.13 = (s32[32]{0:T(128)S(1)}, s32[32]{0:T(128)}, u32[]{:S(2)}) copy-start(s32[32]{0:T(128)} %param.19) | copy-start | bytes 388
  103.1 6.3 %slice-start.2 = ((f32[13288]{0:T(1024)}), f32[1000]{0:T(1024)S(1)}, s32[]{:S(2)}) async-start(f32[13288]{0:T(1024)} %param.29), calls=%async_computation.3 | async-start | bytes 8192 | tf_op jit(solution)/shard_map/slice | solution.py:1673
  103.1 6.9 %copy-start.5 = (f32[13288]{0:T(1024)S(1)}, f32[13288]{0:T(1024)}, u32[]{:S(2)}) copy-start(f32[13288]{0:T(1024)} %param.29) | copy-start | bytes 159460
  111.5 94.1 %copy-start.9 = (s32[2176]{0:T(1024)S(1)}, s32[2176]{0:T(1024)}, u32[]{:S(2)}) copy-start(s32[2176]{0:T(1024)} %param.22) | copy-start | bytes 26116
  111.5 94.1 %copy-start.14 = (s32[2176]{0:T(1024)S(1)}, s32[2176]{0:T(1024)}, u32[]{:S(2)}) copy-start(s32[2176]{0:T(1024)} %constant.101) | copy-start | bytes 26116
  351.9 114.8 %copy-start.8 = (f32[64,128]{1,0:T(8,128)S(1)}, f32[64,128]{1,0:T(8,128)}, u32[]{:S(2)}) copy-start(f32[64,128]{1,0:T(8,128)} %get-tuple-element.96) | copy-start | bytes 98308
  351.9 114.8 %copy-start.3 = (f32[128,1000]{0,1:T(8,128)S(1)}, f32[128,1000]{0,1:T(8,128)}, u32[]{:S(2)}) copy-start(f32[128,1000]{0,1:T(8,128)} %param.28) | copy-start | bytes 1536004
  351.9 114.8 %copy-start.4 = (f32[128,1000]{0,1:T(8,128)S(1)}, f32[128,1000]{0,1:T(8,128)}, u32[]{:S(2)}) copy-start(f32[128,1000]{0,1:T(8,128)} %param.27) | copy-start | bytes 1536004
  462.4 4.3 copy-start.2
  462.4 6.8 %copy-start.6 = (f32[13288]{0:T(1024)S(1)}, f32[13288]{0:T(1024)}, u32[]{:S(2)}) copy-start(f32[13288]{0:T(1024)} %param.31) | copy-start | bytes 159460
  462.4 6.8 %copy-start.7 = (f32[13288]{0:T(1024)S(1)}, f32[13288]{0:T(1024)}, u32[]{:S(2)}) copy-start(f32[13288]{0:T(1024)} %param.30) | copy-start | bytes 159460
  462.4 7.5 %copy-start.1 = (f32[136,4096]{1,0:T(8,128)S(1)}, f32[136,4096]{1,0:T(8,128)}, u32[]{:S(2)}) copy-start(f32[136,4096]{1,0:T(8,128)} %get-tuple-element.125) | copy-start | bytes 6684676
  462.4 8.9 %slice-start = ((s8[4456448]{0:T(1024)(128)(4,1)}), s8[4194304]{0:T(1024)(128)(4,1)S(1)}, s32[]{:S(2)}) async-start(s8[4456448]{0:T(1024)(128)(4,1)} %bitcast.30), calls=%async_computation.1 | async-start | bytes 8388608
  466.7 4.6 slice-start.1
  471.3 3.2 copy-start
Sparse Core Ops, SparseCore 0:
  102.7 77.1 all-gather.2

commit v2 on v1

--- a/solution.py
+++ b/solution.py
@@ -286,7 +286,7 @@
     return high, (v - high.astype(F32)).astype(BF16)
 
 
-def shampoo_rows(final, master, stats, roots, grads, flat, turn, first, group):
+def shampoo_rows(final, updates, stats, roots, grads, flat, turn, first, group):
     for k in range(group):
         rows = pl.ds(k * HALF, HALF)
         parts = [final[h, first + k].astype(F32) for h in range(2)]
@@ -324,9 +324,7 @@
             lanes = pl.ds(p * (BLOCK * BLOCK // 2) + m * LANES, LANES)
             cut = slice(p * BLOCK, (p + 1) * BLOCK)
             grads[here, lanes] = jnp.concatenate([v[:, cut] for v in tiles], axis=1)
-            master[here, lanes] = master[here, lanes] - RATE_SHAMPOO * jnp.concatenate(
-                [v[:, cut] for v in steps], axis=1
-            )
+            updates[here, lanes] = jnp.concatenate([v[:, cut] for v in steps], axis=1)
 
 
 DELIVER_FAR = ()
@@ -336,9 +334,9 @@
 def deliver_kernel(devices, spans, code_ref, head_h, *refs):
     n = len(matrix_list())
     grads, refs = refs[:n], refs[n:]
-    master_h, stats_h, roots_h, head_out, grad_out, stats_out, master_out = refs[:7]
-    pool, acc, land_last, land_mid, land_far, final = refs[7:13]
-    master, stats, roots, grad_flat, flat, turn = refs[13:19]
+    stats_h, roots_h, head_out, grad_out, stats_out, step_out = refs[:6]
+    pool, acc, land_last, land_mid, land_far, final, head_pair = refs[6:13]
+    steps, stats, roots, grad_flat, flat, turn = refs[13:19]
     in_sem, send_sem, last_recv, mid_recv, far_recv, end_send, end_recv, own_sem, out_sem = refs[19:]
     me = lax.axis_index("dp")
     core = lax.axis_index("rows")
@@ -349,9 +347,7 @@
     barrier = pltpu.get_barrier_semaphore()
     for peer in peers:
         pl.semaphore_signal(barrier, inc=1, device_id=peer, device_id_type=MESH_IDS)
-    head = pltpu.make_async_copy(
-        head_h, acc.at[:, pl.ds(count, head_h.shape[1])], in_sem.at[n]
-    )
+    head = pltpu.make_async_copy(head_h, head_pair.at[core], in_sem.at[n])
     head.start()
     loads = []
     start = 0
@@ -361,13 +357,18 @@
         loads.append(load)
         start += grad.shape[0]
     owned = []
-    for i, (src, dst) in enumerate([(stats_h, stats), (roots_h, roots), (master_h, master)]):
+    for i, (src, dst) in enumerate([(stats_h, stats), (roots_h, roots)]):
         load = pltpu.make_async_copy(src, dst, own_sem.at[i])
         load.start()
         owned.append(load)
     pl.semaphore_wait(barrier, len(peers))
     head.wait()
-    sent = []
+    parts = len(spans)
+    sent = [
+        remote(
+            head_pair.at[core], head_pair.at[core], end_send.at[parts], end_recv.at[parts], partner
+        )
+    ]
     stores = []
 
     def store(src, dst):
@@ -379,7 +380,7 @@
         copy = pltpu.make_async_remote_copy(
             src_ref=acc.at[owner, span],
             dst_ref=land.at[at, span],
-            send_sem=send_sem.at[len(sent)],
+            send_sem=send_sem.at[len(sent) - 1],
             recv_sem=sems.at[at, part],
             device_id=device,
             device_id_type=MESH_IDS,
@@ -420,8 +421,7 @@
         lax.fori_loop(0, size, step, 0)
 
     ends = []
-    parts = len(spans)
-    whole_rows = master.shape[0] % 8 != 0
+    whole_rows = steps.shape[0] % 8 != 0
 
     def far_second(part):
         return part in DELIVER_FAR
@@ -431,11 +431,10 @@
         if part < parts:
             first, size = spans[part]
             span = pl.ds(first, size)
-            if part == 1:
+            if part == 0:
                 for load in loads:
                     load.wait()
-            if part > 0:
-                fill(first, size)
+            fill(first, size)
             at = 0
             for q in last[1:]:
                 for m in mid[::-1]:
@@ -529,41 +528,42 @@
             ref = final.at[1 - core, pl.ds(first, size)]
             pltpu.make_async_copy(ref, ref, end_recv.at[part]).wait()
             if part == 0:
-                store(final.at[:, pl.ds(first, size)], head_out)
+                landed(head_pair.at[1 - core], end_recv.at[parts])
+                store(head_pair, head_out)
                 for load in owned:
                     load.wait()
-                continue
 
             def group(i, carry, first=first):
-                shampoo_rows(final, master, stats, roots, grad_flat, flat, turn, first + i * 8, 8)
+                shampoo_rows(final, steps, stats, roots, grad_flat, flat, turn, first + i * 8, 8)
                 return carry
 
             lax.fori_loop(0, size // 8, group, 0)
             if size % 8:
                 shampoo_rows(
-                    final, master, stats, roots, grad_flat, flat, turn, first + size // 8 * 8, size % 8
+                    final, steps, stats, roots, grad_flat, flat, turn, first + size // 8 * 8, size % 8
                 )
             span = pl.ds(first, size)
             store(stats.at[span], stats_out.at[span])
             if not whole_rows:
                 store(grad_flat.at[span], grad_out.at[span])
-                store(master.at[span], master_out.at[span])
+                store(steps.at[span], step_out.at[span])
     if whole_rows:
         store(grad_flat, grad_out)
-        store(master, master_out)
+        store(steps, step_out)
     for copy in sent + ends:
         copy.wait_send()
     for copy in stores:
         copy.wait()
 
 
-def deliver_blocks(grads, head, code, master, stats, roots, devices):
+def deliver_blocks(grads, head, code, stats, roots, devices):
     count = code.shape[0] // devices
-    more = head.shape[1]
-    spans = [(count, more)] + spans_of(count)
+    more = head.shape[0]
+    spans = spans_of(count)
+    flat = (count, BLOCK * BLOCK)
     first, second, third = bit_split(devices)
     n_mid, n_last, n_far = 1 << first, 1 << second, 1 << third
-    tile = (count + more, HALF, LANES)
+    tile = (count, HALF, LANES)
     dma = pltpu.SemaphoreType.DMA
     lands = [(n_last - 1) * n_mid * n_far, (n_mid - 1) * n_far, (n_far - 1) * n_mid]
     grads = [g.reshape(-1, HALF, LANES) for g in grads]
@@ -573,11 +573,11 @@
         functools.partial(deliver_kernel, devices, spans),
         out_shape=[
             jax.ShapeDtypeStruct((2, more, HALF, LANES), BF16),
-            jax.ShapeDtypeStruct(master.shape, F32),
+            jax.ShapeDtypeStruct(flat, F32),
             jax.ShapeDtypeStruct(stats.shape, F32),
-            jax.ShapeDtypeStruct(master.shape, F32),
+            jax.ShapeDtypeStruct(flat, F32),
         ],
-        in_specs=[pl.BlockSpec(memory_space=pltpu.SMEM)] + [any_space] * (4 + len(grads)),
+        in_specs=[pl.BlockSpec(memory_space=pltpu.SMEM)] + [any_space] * (3 + len(grads)),
         out_specs=[any_space] * 4,
         scratch_shapes=[
             pltpu.VMEM((sum(g.shape[0] for g in grads), HALF, LANES), jnp.bfloat16),
@@ -586,10 +586,11 @@
         + [pltpu.VMEM((k,) + tile, jnp.bfloat16) for k in lands]
         + [
             pltpu.VMEM((2,) + tile, jnp.bfloat16),
-            pltpu.VMEM(master.shape, F32),
+            pltpu.VMEM((2, more, HALF, LANES), jnp.bfloat16),
+            pltpu.VMEM(flat, F32),
             pltpu.VMEM(stats.shape, F32),
             pltpu.VMEM(roots.shape, F32),
-            pltpu.VMEM(master.shape, F32),
+            pltpu.VMEM(flat, F32),
             pltpu.VMEM((2, 8 * HALF, LANES), F32),
             pltpu.VMEM((2, 8 * HALF, LANES), F32),
             dma((len(grads) + 1,)),
@@ -597,15 +598,15 @@
             dma((lands[0], steps)),
             dma((lands[1], steps)),
             dma((lands[2], steps)),
-            dma((steps,)),
-            dma((steps,)),
-            dma((3,)),
-            dma((3 * steps,)),
+            dma((steps + 1,)),
+            dma((steps + 1,)),
+            dma((2,)),
+            dma((3 * steps + 3,)),
         ],
         compiler_params=pltpu.CompilerParams(
             collective_id=2, has_side_effects=True, vmem_limit_bytes=60 * 2**20
         ),
-    )(code, head, *grads, master, stats, roots)
+    )(code, head, *grads, stats, roots)
 
 
 def block_places(owner_slot):
@@ -657,21 +658,32 @@
         self.near_slots = [self.near_at ^ m for m in range(1, self.near)]
         self.far_peers = [(self.me ^ (m * self.near), self.core) for m in range(1, self.far)]
         self.far_slots = [self.far_at ^ m for m in range(1, self.far)]
+        self.direct = devices <= DIRECT
+        self.all_slots = [self.me ^ m for m in range(1, devices)]
+        self.all_peers = [(slot, self.core) for slot in self.all_slots]
+        self.devices = devices
+
+    def known(self):
+        if self.direct:
+            return [self.partner] + self.all_peers
+        return [self.partner] + self.near_peers + self.far_peers
 
     def hello(self):
         barrier = pltpu.get_barrier_semaphore()
-        for peer in [self.partner] + self.near_peers + self.far_peers:
+        for peer in self.known():
             pl.semaphore_signal(barrier, inc=1, device_id=peer, device_id_type=MESH_IDS)
 
     def ready(self):
-        pl.semaphore_wait(
-            pltpu.get_barrier_semaphore(), 1 + len(self.near_peers) + len(self.far_peers)
-        )
+        pl.semaphore_wait(pltpu.get_barrier_semaphore(), len(self.known()))
+
+
+DIRECT = 16
 
 
 def slots_total(devices):
     first, second, third = bit_split(devices)
-    return 2 + (1 << (first + second)) + (1 << third)
+    staged = 2 + (1 << (first + second)) + (1 << third)
+    return max(staged, 2 + devices) if devices <= DIRECT else staged
 
 
 def remote(src, dst, send_sem, recv_sem, device):
@@ -719,12 +731,16 @@
 
 def reduce_all(net, value, bufs, send_sem, recv_sem, merge, own_count=None, pair_count=0.0, fillers=()):
     fillers = list(fillers) + [None] * 3
+    fillers_after = fillers[1:]
     copies = []
     stages = [
         (0, net.core, [net.partner], [1 - net.core], 2),
         (2, net.near_at, net.near_peers, net.near_slots, net.near),
         (2 + net.near, net.far_at, net.far_peers, net.far_slots, net.far),
     ]
+    if net.direct and value.shape[0] <= 2 * N_MID:
+        stages = stages[:1] + [(2, net.me, net.all_peers, net.all_slots, net.devices)]
+        fillers = [fillers[0], lambda: [more() for more in fillers_after if more is not None]]
     for step, (base, mine, peers, slots, size) in enumerate(stages):
         bufs[base + mine] = value
         for i, peer in enumerate(peers):
@@ -1237,6 +1253,7 @@
     take = lambda n: [refs.pop(0) for _ in range(n)]
     names = ["zc", "hb", "hp", "zb", "za", "wi", "wm", "wo"]
     source = {}
+    head_h, = take(1)
     source["xf", 1], source["xb", 1] = take(2)
     for at in (0, 1):
         for name in names:
@@ -1246,14 +1263,17 @@
     params_of = take(LAYERS)
     live, extra = take(2)
     out_of = [take(3) for _ in range(LAYERS)]
+    head_out, = take(1)
     small_of = take(LAYERS)
     field, xb, zc, hb, hp, zb, za, wi, wm, wo = take(10)
     place = dict(xf=field, xb=xb, zc=zc, hb=hb, hp=hp, zb=zb, za=za, wi=wi, wm=wm, wo=wo)
     g_side, g_mid, r_side, r_mid = take(4)
     ec, ep, ea, ub = take(4)
+    head, land_last, land_mid, land_far = take(4)
     stage_m, stage_c = take(2)
     bufs_of = [take(3) for _ in range(LAYERS)]
     in_sem, out_sem, send_sem, recv_sem, halo_sem, pair_sem = take(6)
+    head_in, head_send, last_recv, mid_recv, far_recv = take(5)
 
     net = Net(devices)
     net.hello()
@@ -1272,6 +1292,8 @@
 
     for name in order:
         start(name, 1)
+    head_load = pltpu.make_async_copy(head_h, head, head_in)
+    head_load.start()
     clear_edges(ep, net.core)
     quarter = za.shape[1] // ROW_SLOTS
     batch = quarter // WIDTH
@@ -1313,6 +1335,72 @@
 
         lax.fori_loop(0, grad.shape[0] // 16, step, 0)
         return store(other, out)
+
+    mid, last, far = axis_masks(devices, net.core)
+    me, core = net.me, net.core
+    head_sent = []
+
+    def head_copy(owner, land, sems, slot, device):
+        head_sent.append(
+            remote(head.at[owner], land.at[slot], head_send.at[len(head_sent)], sems.at[slot], device)
+        )
+
+    def head_add(owners, land, sems):
+        for slot in range(len(owners)):
+            landed(land.at[slot], sems.at[slot])
+
+        def step(i, carry):
+            for slot, owner in enumerate(owners):
+                head[owner, i] = (
+                    head[owner, i].astype(F32) + land[slot, i].astype(F32)
+                ).astype(BF16)
+            return carry
+
+        lax.fori_loop(0, head.shape[1], step, 0)
+
+    def head_first():
+        head_load.wait()
+        slot = 0
+        for q in last[1:]:
+            for m in mid:
+                for z in far:
+                    head_copy(me ^ q ^ m ^ z, land_last, last_recv, slot, (me ^ q, core))
+                    slot += 1
+
+    def head_second():
+        owners = [me ^ m ^ z for m in mid for z in far]
+        for j in range(len(last) - 1):
+            view = pl.ds(j * len(owners), len(owners))
+            head_add(owners, land_last.at[view], last_recv.at[view])
+        slot = 0
+        for m in mid[1:]:
+            for z in far:
+                head_copy(me ^ m ^ z, land_mid, mid_recv, slot, (me ^ m, core))
+                slot += 1
+
+    def head_third():
+        owners = [me ^ z for z in far]
+        for j in range(len(mid) - 1):
+            view = pl.ds(j * len(owners), len(owners))
+            head_add(owners, land_mid.at[view], mid_recv.at[view])
+        for slot, z in enumerate(far[1:]):
+            head_copy(me ^ z, land_far, far_recv, slot, (me ^ z, core))
+
+    def head_last():
+        for slot in range(len(far) - 1):
+            landed(land_far.at[slot], far_recv.at[slot])
+
+        def step(i, carry):
+            total = head[me, i].astype(F32)
+            for slot in range(len(far) - 1):
+                total = total + land_far[slot, i].astype(F32)
+            head[me, i] = total.astype(BF16)
+            return carry
+
+        lax.fori_loop(0, head.shape[1], step, 0)
+        for copy in head_sent:
+            copy.wait_send()
+        return store(head.at[me], head_out)
 
     def layer(at, fillers):
         top = at == 1
@@ -1373,6 +1461,8 @@
             stage_c[2 * N_IN :] = jnp.zeros(extra.shape, F32)
         total_c = totals(stage_c, 2, 4 * N_MID, N_IN, fillers)
         small[4 * N_MID + 2 * N_IN :] = total_c[2 * N_IN :]
+        if not top:
+            head_third()
 
         def back_c(j, carry):
             mean, scale = row(stat_c, j), row(stat_c, N_IN + j)
@@ -1439,6 +1529,8 @@
         )
         refill("hb")
         out_swap = swap(g_side, r_side, at, 0)
+        if top:
+            head_first()
 
         def fill_b(slot):
             rows = pl.ds(slot * quarter, quarter)
@@ -1498,6 +1590,8 @@
         totals(stage_m, 0, 0, N_MID, [grad_mid(0, 2), grad_mid(2, 5), grad_mid(5, 9)])
         refill("hp")
         mid_swap = swap(g_mid, r_mid, at, 1)
+        if top:
+            head_second()
 
         def fill_a(j, carry):
             for q in range(4):
@@ -1552,13 +1646,16 @@
         return [first_part, second_part, third_part]
 
     rest = layer(1, [])
-    for step in layer(0, rest):
+    final = layer(0, rest)
+    head_store = head_last()
+    for step in final:
         step()
+    head_store.wait()
     for copy in sends:
         copy.wait_send()
 
 
-def backward_pass(devices, total_count, xf, xb, kept, weights, x, gtop, params, live, extra):
+def backward_pass(devices, total_count, head, xf, xb, kept, weights, x, gtop, params, live, extra):
     shape = jax.ShapeDtypeStruct
     any_space = pl.BlockSpec(memory_space=pl.ANY)
     vmem = pl.BlockSpec(memory_space=pltpu.VMEM)
@@ -1570,11 +1667,14 @@
     for at in range(LAYERS):
         za, hp, zb, hb, zc = kept[at][:5]
         each.append([zc, hb, hp, zb, za] + list(weights[3 * at : 3 * at + 3]))
-    ins = [xf, xb] + each[0] + each[1]
+    ins = [head, xf, xb] + each[0] + each[1]
     small_ins = [x, gtop]
     for at in range(LAYERS):
         small_ins += kept[at][5:]
     small_ins += list(params) + [live, extra]
+    first, second, third = bit_split(devices)
+    n_mid, n_last, n_far = 1 << first, 1 << second, 1 << third
+    lands = [(n_last - 1) * n_mid * n_far, (n_mid - 1) * n_far, n_far - 1]
     side = N_IN * M // 32
     middle = N_MID * 9 * M // 32
     small_rows = 4 * N_MID + 2 * N_IN + extra.shape[0]
@@ -1582,9 +1682,11 @@
     grads = [shape((n, HALF, LANES), BF16) for n in (side, middle, side)]
     out = pl.pallas_call(
         functools.partial(backward_kernel, devices, total_count),
-        out_shape=grads * LAYERS + [shape((small_rows, LANES), F32)] * LAYERS,
+        out_shape=grads * LAYERS
+        + [shape(head.shape[1:], BF16)]
+        + [shape((small_rows, LANES), F32)] * LAYERS,
         in_specs=[any_space] * len(ins) + [vmem] * len(small_ins),
-        out_specs=[any_space] * (3 * LAYERS) + [vmem] * LAYERS,
+        out_specs=[any_space] * (3 * LAYERS + 1) + [vmem] * LAYERS,
         scratch_shapes=[big(a) for a in [xf, xb] + each[0]]
         + [
             pltpu.VMEM((side, 2, HALF, LANES), BF16),
@@ -1595,23 +1697,32 @@
             pltpu.VMEM(kept[0][1].shape, BF16),
             pltpu.VMEM((N_MID, rows, LANES), BF16),
             pltpu.VMEM((N_MID, rows, LANES), F32),
+            big(head),
+        ]
+        + [pltpu.VMEM((n,) + head.shape[1:], BF16) for n in lands]
+        + [
             pltpu.VMEM((2 * N_MID, LANES), F32),
             pltpu.VMEM((stage_rows[2], LANES), F32),
         ]
         + [pltpu.VMEM((total, n, LANES), F32) for n in stage_rows] * LAYERS
         + [
             dma((LAYERS, 10)),
-            dma((3 * LAYERS,)),
+            dma((3 * LAYERS + 1,)),
             dma((3 * LAYERS, total)),
             dma((3 * LAYERS, total)),
             dma((LAYERS, 2)),
             dma((LAYERS, 2, 3)),
+            dma(()),
+            dma((sum(lands),)),
+            dma((lands[0],)),
+            dma((lands[1],)),
+            dma((lands[2],)),
         ],
         compiler_params=pltpu.CompilerParams(
             collective_id=6, has_side_effects=True, vmem_limit_bytes=62 * 2**20
         ),
     )(*ins, *small_ins)
-    return out[: 3 * LAYERS], out[3 * LAYERS :]
+    return out[: 3 * LAYERS], out[3 * LAYERS], out[3 * LAYERS + 1 :]
 
 
 def adamw(values_old, gradient, moment_one, moment_two, step_rate):
@@ -1714,18 +1825,18 @@
             .transpose(1, 0, 2)
             .reshape(devices, head_blocks, HALF, LANES)
         )
-    grads, (small_bottom, small_top) = backward_pass(
-        devices, live_count, field, low, kept, weights, first, g_top, params, live_rows, extra
+    grads, head_mine, (small_bottom, small_top) = backward_pass(
+        devices, live_count, grad_head, field, low, kept, weights, first, g_top, params, live_rows, extra
     )
-    head_sum, conv_grad, stats_new, master_new = deliver_blocks(
+    head_sum, conv_grad, stats_new, step = deliver_blocks(
         grads,
-        grad_head,
+        head_mine,
         block_places(owner_slot),
-        conv_master,
         conv_stats,
         conv_roots,
         devices,
     )
+    master_new = conv_master - RATE_SHAMPOO * step
     head_grad = head_sum.reshape(WIDE, head_rows)[:CLASSES].T.astype(F32)
     head_one, head_two, head_new = adamw(
         head_master, head_grad, head_moment_one, head_moment_two, RATE_HEAD

time: 492 us -> 477 us (0.970)
  Pallas kernels: 434 us -> 420 us
    pallas_call x1, Pallas kernels: 110 us -> 97.9 us  [deliver_blocks(): pl.pallas_call(functools.partial(deliver_kernel, devices, spans), out_sha...]
  transfers between devices with their start and end apart: 1 -> 1, of which waited for: 0 -> 0; matrix products, arithmetic and copies ran while one was open for 3% -> 4% of each run, Pallas kernels for 19% -> 19%
where the time goes in v2:
time: 477 us; the launch traced here: 468 us
  Pallas kernels  420 us (88%)
  local copies, waits for them, and re-layouts  16.5 us (3%)
  other arithmetic  16 us (3%)
  between operations  14.7 us (3%)
    pallas_call x1, Pallas kernels, backward_pass(): pl.pallas_call(functools.partial(backward_kernel, devices, total_count),...  108 us
    pallas_call x1, Pallas kernels, deliver_blocks(): pl.pallas_call(functools.partial(deliver_kernel, devices, spans), out_sha...  97.9 us
    pallas_call x1, Pallas kernels, bring_weights(): pl.pallas_call(functools.partial(bring_kernel, devices, spans), out_shape...  92.2 us
    pallas_call x1, Pallas kernels, forward_pass(): pl.pallas_call(functools.partial(forward_kernel, devices, total_count), o...  87.3 us
    pallas_call x1, Pallas kernels, head_step(): pl.pallas_call(functools.partial(head_kernel, devices, float(HEIGHT * WID...  34.9 us
  transfers between devices with their start and end apart: 1, of which 0 were waited for; matrix products, arithmetic and copies ran while one was open for 4% of the time, Pallas kernels for 19%

profile of v2, /device:TPU:0, one launch (start us, length us, event | category | flops | bytes accessed | tf_op | source)
XLA Modules:
  0.0 467.7 jit_solution(15126119490239509418)
XLA Ops:
  7.2 0.0 copy-start.10
  7.2 0.0 copy-start.11
  7.2 0.0 copy-start.12
  7.2 0.0 all-gather.3.cloned.1.call-start
  7.3 1.3 fusion.5.idx_ref
  8.6 1.1 convert_bitcast_fusion
  9.6 92.2 %shard_map.264 = (bf16[4,2048,128]{2,1,0:T(8,128)(2,1)}, bf16[4,4608,128]{2,1,0:T(8,128)(2,1)}, bf16[16,512,128]{2,1,0:T(8,128)(2,1)}, bf16[4,2048,128]{2,1,0:T(...) custom-call(s32[2176]{0:T(1024)} %fusion.5.idx_ref, f32[136,4096]{1,0:T(8,128)} %m_ref.1), custom_call_target="tpu_custom_call" | custom-call | tf_op jit(solution)/shard_map/pallas_call | solution.py:262
  101.9 0.7 pad.8
  102.6 0.0 all-gather.3.cloned.1.call-update
  102.6 0.0 copy-done.10
  102.7 0.1 reshape.191
  102.7 0.1 dynamic_slice.10
  102.8 0.0 copy-done.11
  102.8 0.1 reshape.190
  102.9 0.1 dynamic_slice.9
  103.0 0.0 copy-done.12
  103.0 0.1 and_convert_fusion
  103.1 0.1 broadcast_in_dim.75
  103.2 5.9 %copy.35 = bf16[4,7,32,2048]{3,2,1,0:T(8,128)(2,1)} copy(bf16[4,7,32,2048]{3,0,1,2:T(4,128)(2,1)} %bitcast.33) | data formatting | bytes 7340032 | tf_op jit(solution)/shard_map/transpose | solution.py:1779
  109.1 0.1 mul.117
  109.2 0.1 eq.83
  109.3 0.1 reshape.189
  109.4 0.0 copy-done.13
  109.4 0.1 dynamic_slice.11
  109.4 0.0 slice-done.2
  109.4 0.6 pad.9
  110.0 0.0 copy-done.6
  110.0 0.6 slice_bitcast_fusion.2
  110.7 1.0 broadcast_in_dim.76.refs_9_.refs_29_
  111.6 87.3 %shard_map.265 = (f32[4,896,128]{2,1,0:T(8,128)}, bf16[4,6,9,32,128]{4,3,2,1,0:T(8,128)(2,1)}, f32[4,896,128]{2,1,0:T(8,128)}, bf16[4,896,128]{2,1,0:T(8,128)(2,...) custom-call(bf16[4,2048,128]{2,1,0:T(8,128)(2,1)} %get-tuple-element, ...), custom_call_target="tpu_custom_call" | custom-call | tf_op jit(solution)/shard_map/pallas_call | solution.py:1060
  199.0 0.6 convert_reduce_fusion
  199.6 0.2 select_reduce_fusion.1
  199.8 1.3 select_select_fusion.numbers
  201.1 0.7 compare_convert_fusion.pick
  201.7 0.7 select_convert_fusion.point
  202.4 0.7 fusion.2.hot
  203.1 0.0 copy-done.9
  203.1 0.0 copy-done.14
  203.1 3.3 select_reduce_fusion.code_ref
  206.5 34.9 %shard_map.266 = (f32[16,128]{1,0:T(8,128)}, f32[16,32,128]{2,1,0:T(8,128)}, bf16[16,32,16,128]{3,2,1,0:T(8,128)(2,1)}) custom-call(f32[16,32,128]{2,1,0:T(8,128)} %get-tuple-element.63.pooled, bf16[16,1024,128]{2,1,0:T(8,128)(2,1)} %bitcast.32, f32[1,1024]{1,0:T(1,128)} %bitcast.38, bf16[16,512]{1,0:T(8,128)(2,1)} %compare_convert_fusion.pick, ...), custom_call_target="tpu_custom_call" | custom-call | tf_op jit(solution)/shard_map/pallas_call | solution.py:1215
  241.3 108.0 %shard_map.267 = (bf16[256,16,128]{2,1,0:T(8,128)(2,1)}, bf16[576,16,128]{2,1,0:T(8,128)(2,1)}, bf16[256,16,128]{2,1,0:T(8,128)(2,1)}, bf16[256,16,128]{2,1,0:T(...) custom-call(bf16[16,32,16,128]{3,2,1,0:T(8,128)(2,1)} %get-tuple-ele, ...), custom_call_target="tpu_custom_call" | custom-call | tf_op jit(solution)/shard_map/pallas_call | solution.py:1683
  349.3 0.7 slice_bitcast_fusion
  350.1 0.7 slice_bitcast_fusion.4
  350.8 1.2 slice.30
  351.9 0.7 slice_bitcast_fusion.1
  352.7 97.9 %shard_map.268 = (bf16[2,32,16,128]{3,2,1,0:T(8,128)(2,1)}, f32[136,4096]{1,0:T(8,128)}, f32[136,64,128]{2,1,0:T(8,128)}, f32[136,4096]{1,0:T(8,128)}) custom-call(s32[2176]{0:T(1024)} %select_reduce_fusion.code_ref, bf16[32,16,128]{2,1,0:T(8,128)(2,1)} %get-tuple-element.87.head_h, bf16[256,16,128]{2,1,0:T(8,128)(2,1)} %get-tuple-element.88.refs_0_, ...), custom_call_target="tpu_custom_call" | custom-call | tf_op jit(solution)/shard_map/pallas_call | solution.py:572
  450.6 0.0 copy-done
  450.6 0.0 copy-start.2
  450.6 0.0 copy-start.3
  450.7 0.0 copy-start.4
  450.7 0.0 copy-start.5
  450.7 0.0 slice-start
  450.7 3.9 fusion.11
  454.6 0.0 copy-done.2
  454.6 0.0 copy-done.3
  454.6 0.0 copy-done.4
  454.6 0.0 copy-done.5
  454.6 0.0 slice-start.1
  454.6 1.5 fusion.8
  456.1 0.7 multiply_subtract_fusion.2
  456.8 0.1 copy-done.1
  456.9 1.4 copy.40
  458.3 0.0 slice-done.1
  458.3 2.1 copy.41
  (23 shorter events, 0.1 us)
Async XLA Ops:
  7.2 95.5 %copy-start.10 = (s32[512]{0:T(512)S(1)}, s32[512]{0:T(512)}, u32[]{:S(2)}) copy-start(s32[512]{0:T(512)} %param.21) | copy-start | bytes 6148
  7.2 95.6 %copy-start.11 = (s32[512]{0:T(512)S(1)}, s32[512]{0:T(512)}, u32[]{:S(2)}) copy-start(s32[512]{0:T(512)} %param.20) | copy-start | bytes 6148
  7.2 95.8 %copy-start.12 = (s32[32]{0:T(128)S(1)}, s32[32]{0:T(128)}, u32[]{:S(2)}) copy-start(s32[32]{0:T(128)} %param.18) | copy-start | bytes 388
  7.2 199.3 %all-gather.3.cloned.1.call-start = ((), (), s32[]{:S(2)}) async-start(), calls=%async_computation | async-start | bytes 4456448 | tf_op jit(solution)/shard_map/all_gather | solution.py:1768
  103.2 6.2 %copy-start.13 = (s32[32]{0:T(128)S(1)}, s32[32]{0:T(128)}, u32[]{:S(2)}) copy-start(s32[32]{0:T(128)} %param.19) | copy-start | bytes 388
  103.2 6.3 %slice-start.2 = ((f32[13288]{0:T(1024)}), f32[1000]{0:T(1024)S(1)}, s32[]{:S(2)}) async-start(f32[13288]{0:T(1024)} %param.29), calls=%async_computation.3 | async-start | bytes 8192 | tf_op jit(solution)/shard_map/slice | solution.py:1784
  103.2 6.9 %copy-start.6 = (f32[13288]{0:T(1024)S(1)}, f32[13288]{0:T(1024)}, u32[]{:S(2)}) copy-start(f32[13288]{0:T(1024)} %param.29) | copy-start | bytes 159460
  111.6 91.5 %copy-start.9 = (s32[2176]{0:T(1024)S(1)}, s32[2176]{0:T(1024)}, u32[]{:S(2)}) copy-start(s32[2176]{0:T(1024)} %param.22) | copy-start | bytes 26116
  111.6 91.5 %copy-start.14 = (s32[2176]{0:T(1024)S(1)}, s32[2176]{0:T(1024)}, u32[]{:S(2)}) copy-start(s32[2176]{0:T(1024)} %constant.103) | copy-start | bytes 26116
  352.7 97.9 %copy-start = (f32[136,4096]{1,0:T(8,128)S(1)}, f32[136,4096]{1,0:T(8,128)}, u32[]{:S(2)}) copy-start(f32[136,4096]{1,0:T(8,128)} %m_ref.1) | copy-start | bytes 6684676
  450.6 3.9 copy-start.2
  450.6 3.9 copy-start.3
  450.7 3.9 copy-start.4
  450.7 3.9 copy-start.5
  450.7 7.6 %slice-start = ((s8[4456448]{0:T(1024)(128)(4,1)}), s8[4194304]{0:T(1024)(128)(4,1)S(1)}, s32[]{:S(2)}) async-start(s8[4456448]{0:T(1024)(128)(4,1)} %bitcast.30), calls=%async_computation.1 | async-start | bytes 8388608
  454.6 1.6 copy-start.7
  454.6 1.6 copy-start.8
  454.6 2.3 copy-start.1
  454.6 3.7 slice-start.1
Sparse Core Ops, SparseCore 0:
  102.7 80.3 all-gather.2

commit v3 on v2

--- a/solution.py
+++ b/solution.py
@@ -1085,11 +1085,13 @@
 
 
 def head_kernel(
-    devices, area, pooled, head_h, bias, pick, point, numbers, hot,
-    extra, gtop, gh_h,
+    devices, area, emit, pooled, head_h, bias, pick, point, numbers, hot, extra, gtop, *refs
+):
+    outs, refs = (refs[:1], refs[1:]) if emit else (refs[:2], refs[2:])
+    (
     head, send_pool, recv_pool, low, logits_all, logits, g_low, gh, gh_there, gh_other, gt,
     in_sem, out_sem, send_sem, recv_sem,
-):
+    ) = refs
     net = Net(devices)
     net.hello()
     load = pltpu.make_async_copy(head_h, head, in_sem)
@@ -1169,40 +1171,47 @@
         )
     )
 
-    at += 1
-    block = (WIDE // 2 // HALF, HALF, LANES)
-    cut = WIDE // 2
-    mine_at = pl.multiple_of(net.core * cut, cut)
-    theirs_at = pl.multiple_of((1 - net.core) * cut, cut)
-
-    def grad_there(j, carry):
-        part = dot(g_low[:, pl.ds(theirs_at, cut)], low[j], 0, 0)
-        gh_there[j] = part.astype(BF16).reshape(block)
-        return carry
-
-    lax.fori_loop(0, N_IN, grad_there, 0)
-    sends.append(
-        remote(gh_there, gh_other, send_sem.at[at], recv_sem.at[3 + net.near + net.far], net.partner)
-    )
+    if emit:
+        at += 1
+        block = (WIDE // 2 // HALF, HALF, LANES)
+        cut = WIDE // 2
+        mine_at = pl.multiple_of(net.core * cut, cut)
+        theirs_at = pl.multiple_of((1 - net.core) * cut, cut)
+
+        def grad_there(j, carry):
+            part = dot(g_low[:, pl.ds(theirs_at, cut)], low[j], 0, 0)
+            gh_there[j] = part.astype(BF16).reshape(block)
+            return carry
+
+        lax.fori_loop(0, N_IN, grad_there, 0)
+        sends.append(
+            remote(
+                gh_there, gh_other, send_sem.at[at], recv_sem.at[3 + net.near + net.far], net.partner
+            )
+        )
+    else:
+        outs[0][...] = low[...].astype(F32)
+        outs[1][...] = g_low[...].astype(F32)
     landed(gt.at[:, 1 - net.core], recv_sem.at[2 + net.near + net.far])
     for j in range(N_IN):
         gtop[j] = jnp.concatenate([gt[j, 0], gt[j, 1]], axis=0).astype(F32)
-    landed(gh_other, recv_sem.at[3 + net.near + net.far])
-
-    def grad_here(j, carry):
-        part = dot(g_low[:, pl.ds(mine_at, cut)], low[j], 0, 0)
-        gh[j] = (part.reshape(block) + gh_other[j].astype(F32)).astype(BF16)
-        return carry
-
-    lax.fori_loop(0, N_IN, grad_here, 0)
-    store = pltpu.make_async_copy(gh, gh_h, out_sem)
-    store.start()
-    store.wait()
+    if emit:
+        landed(gh_other, recv_sem.at[3 + net.near + net.far])
+
+        def grad_here(j, carry):
+            part = dot(g_low[:, pl.ds(mine_at, cut)], low[j], 0, 0)
+            gh[j] = (part.reshape(block) + gh_other[j].astype(F32)).astype(BF16)
+            return carry
+
+        lax.fori_loop(0, N_IN, grad_here, 0)
+        store = pltpu.make_async_copy(gh, outs[0], out_sem)
+        store.start()
+        store.wait()
     for copy in sends:
         copy.wait_send()
 
 
-def head_step(devices, pooled, head, bias, pick, point, numbers, hot):
+def head_step(devices, emit, pooled, head, bias, pick, point, numbers, hot):
     batch = pooled.shape[1]
     half = batch // 2
     shape = jax.ShapeDtypeStruct
@@ -1213,14 +1222,18 @@
     first, second, third = bit_split(devices)
     near, far = 1 << (first + second), 1 << third
     return pl.pallas_call(
-        functools.partial(head_kernel, devices, float(HEIGHT * WIDTH)),
+        functools.partial(head_kernel, devices, float(HEIGHT * WIDTH), emit),
         out_shape=[
             shape((16, LANES), F32),
             shape((N_IN, batch, LANES), F32),
-            shape((N_IN, WIDE // 2 // HALF, HALF, LANES), BF16),
-        ],
+        ]
+        + (
+            [shape((N_IN, WIDE // 2 // HALF, HALF, LANES), BF16)]
+            if emit
+            else [shape((N_IN, half, LANES), F32), shape((half, WIDE), F32)]
+        ),
         in_specs=[vmem, any_space] + [vmem] * 5,
-        out_specs=[vmem, vmem, any_space],
+        out_specs=[vmem, vmem] + ([any_space] if emit else [vmem, vmem]),
         scratch_shapes=[
             pltpu.VMEM((N_IN, WIDE, LANES), BF16),
             pltpu.VMEM((N_IN, half, LANES), BF16),
@@ -1248,12 +1261,12 @@
     return part[:, j * LANES : (j + 1) * LANES].astype(BF16).reshape(-1, 2, HALF, LANES)
 
 
-def backward_kernel(devices, total_count, *refs):
+def backward_kernel(devices, total_count, inside, *refs):
     refs = list(refs)
     take = lambda n: [refs.pop(0) for _ in range(n)]
     names = ["zc", "hb", "hp", "zb", "za", "wi", "wm", "wo"]
     source = {}
-    head_h, = take(1)
+    head_h, = [None] if inside else take(1)
     source["xf", 1], source["xb", 1] = take(2)
     for at in (0, 1):
         for name in names:
@@ -1262,6 +1275,7 @@
     stats_of = [take(3) for _ in range(LAYERS)]
     params_of = take(LAYERS)
     live, extra = take(2)
+    low, g_low = take(2) if inside else [None, None]
     out_of = [take(3) for _ in range(LAYERS)]
     head_out, = take(1)
     small_of = take(LAYERS)
@@ -1273,7 +1287,7 @@
     stage_m, stage_c = take(2)
     bufs_of = [take(3) for _ in range(LAYERS)]
     in_sem, out_sem, send_sem, recv_sem, halo_sem, pair_sem = take(6)
-    head_in, head_send, last_recv, mid_recv, far_recv = take(5)
+    head_in, head_send, last_recv, mid_recv, far_recv, swap_sem = take(6)
 
     net = Net(devices)
     net.hello()
@@ -1292,8 +1306,9 @@
 
     for name in order:
         start(name, 1)
-    head_load = pltpu.make_async_copy(head_h, head, head_in)
-    head_load.start()
+    if not inside:
+        head_load = pltpu.make_async_copy(head_h, head, head_in)
+        head_load.start()
     clear_edges(ep, net.core)
     quarter = za.shape[1] // ROW_SLOTS
     batch = quarter // WIDTH
@@ -1358,8 +1373,44 @@
 
         lax.fori_loop(0, head.shape[1], step, 0)
 
+    cut = WIDE // 2
+    lot = cut // (2 * HALF)
+    state = {}
+
+    def head_part(j, which):
+        classes = pl.ds(pl.multiple_of(which * cut, cut), cut)
+        return dot(g_low[:, classes].astype(BF16), low[j].astype(BF16), 0, 0)
+
+    def head_there():
+        def step(j, carry):
+            part = head_part(j, 1 - core).astype(BF16)
+            g_mid[pl.ds(j * lot, lot)] = part.reshape(lot, 2, HALF, LANES)
+            return carry
+
+        lax.fori_loop(0, N_IN, step, 0)
+        state["there"] = remote(
+            g_mid.at[pl.ds(0, N_IN * lot)],
+            g_mid.at[pl.ds(N_IN * lot, N_IN * lot)],
+            swap_sem.at[0],
+            swap_sem.at[1],
+            net.partner,
+        )
+
+    def head_here():
+        landed(g_mid.at[pl.ds(N_IN * lot, N_IN * lot)], swap_sem.at[1])
+
+        def step(j, carry):
+            other = g_mid[pl.ds((N_IN + j) * lot, lot)].astype(F32)
+            part = head_part(j, core).reshape(lot, 2, HALF, LANES) + other
+            head[j] = part.astype(BF16).reshape(2 * lot, HALF, LANES)
+            return carry
+
+        lax.fori_loop(0, N_IN, step, 0)
+        state["there"].wait_send()
+
     def head_first():
-        head_load.wait()
+        if not inside:
+            head_load.wait()
         slot = 0
         for q in last[1:]:
             for m in mid:
@@ -1645,7 +1696,7 @@
 
         return [first_part, second_part, third_part]
 
-    rest = layer(1, [])
+    rest = layer(1, [head_there, None, head_here] if inside else [])
     final = layer(0, rest)
     head_store = head_last()
     for step in final:
@@ -1667,11 +1718,15 @@
     for at in range(LAYERS):
         za, hp, zb, hb, zc = kept[at][:5]
         each.append([zc, hb, hp, zb, za] + list(weights[3 * at : 3 * at + 3]))
-    ins = [head, xf, xb] + each[0] + each[1]
+    inside = len(head) == 2
+    head_shape = shape((devices, WIDE // 2 // HALF, HALF, LANES), BF16)
+    if not inside:
+        head_shape = shape(head[0].shape, BF16)
+    ins = ([] if inside else list(head)) + [xf, xb] + each[0] + each[1]
     small_ins = [x, gtop]
     for at in range(LAYERS):
         small_ins += kept[at][5:]
-    small_ins += list(params) + [live, extra]
+    small_ins += list(params) + [live, extra] + (list(head) if inside else [])
     first, second, third = bit_split(devices)
     n_mid, n_last, n_far = 1 << first, 1 << second, 1 << third
     lands = [(n_last - 1) * n_mid * n_far, (n_mid - 1) * n_far, n_far - 1]
@@ -1681,9 +1736,9 @@
     stage_rows = [2 * N_MID, 2 * N_MID, 2 * N_IN + extra.shape[0]]
     grads = [shape((n, HALF, LANES), BF16) for n in (side, middle, side)]
     out = pl.pallas_call(
-        functools.partial(backward_kernel, devices, total_count),
+        functools.partial(backward_kernel, devices, total_count, inside),
         out_shape=grads * LAYERS
-        + [shape(head.shape[1:], BF16)]
+        + [shape(head_shape.shape[1:], BF16)]
         + [shape((small_rows, LANES), F32)] * LAYERS,
         in_specs=[any_space] * len(ins) + [vmem] * len(small_ins),
         out_specs=[any_space] * (3 * LAYERS + 1) + [vmem] * LAYERS,
@@ -1697,9 +1752,9 @@
             pltpu.VMEM(kept[0][1].shape, BF16),
             pltpu.VMEM((N_MID, rows, LANES), BF16),
             pltpu.VMEM((N_MID, rows, LANES), F32),
-            big(head),
+            big(head_shape),
         ]
-        + [pltpu.VMEM((n,) + head.shape[1:], BF16) for n in lands]
+        + [pltpu.VMEM((n,) + head_shape.shape[1:], BF16) for n in lands]
         + [
             pltpu.VMEM((2 * N_MID, LANES), F32),
             pltpu.VMEM((stage_rows[2], LANES), F32),
@@ -1717,6 +1772,7 @@
             dma((lands[0],)),
             dma((lands[1],)),
             dma((lands[2],)),
+            dma((2,)),
         ],
         compiler_params=pltpu.CompilerParams(
             collective_id=6, has_side_effects=True, vmem_limit_bytes=62 * 2**20
@@ -1806,8 +1862,10 @@
     numbers = jnp.where(
         lane == 0, own_weight[:, None], jnp.where(lane == 1, in_weight[:, None], weight_total)
     )
-    extra, g_top, grad_head = head_step(
+    emit = head_rows != LANES
+    extra, g_top, *grad_head = head_step(
         devices,
+        emit,
         pooled,
         head_all,
         bias,
@@ -1817,9 +1875,9 @@
         hot,
     )
     head_blocks = head_rows // 4
-    if head_rows != LANES:
-        grad_head = (
-            grad_head.reshape(N_IN, WIDE // 2, LANES)
+    if emit:
+        grad_head[0] = (
+            grad_head[0].reshape(N_IN, WIDE // 2, LANES)
             .transpose(1, 0, 2)
             .reshape(WIDE // 2, devices, head_rows)
             .transpose(1, 0, 2)

time: 477 us -> 468 us (0.981)
  Pallas kernels: 420 us -> 411 us
    pallas_call x1, Pallas kernels: 34.9 us -> 23.3 us  [head_step(): pl.pallas_call(functools.partial(head_kernel, devices, float(HEIGHT * WID...]
where the time goes in v3:
time: 468 us; the launch traced here: 459 us
  Pallas kernels  411 us (88%)
  local copies, waits for them, and re-layouts  16.5 us (4%)
  other arithmetic  16 us (3%)
  between operations  14.7 us (3%)
    pallas_call x1, Pallas kernels, backward_pass(): pl.pallas_call(functools.partial(backward_kernel, devices, total_count, i...  111 us
    pallas_call x1, Pallas kernels, deliver_blocks(): pl.pallas_call(functools.partial(deliver_kernel, devices, spans), out_sha...  97.8 us
    pallas_call x1, Pallas kernels, bring_weights(): pl.pallas_call(functools.partial(bring_kernel, devices, spans), out_shape...  92.2 us
    pallas_call x1, Pallas kernels, forward_pass(): pl.pallas_call(functools.partial(forward_kernel, devices, total_count), o...  87.3 us
    pallas_call x1, Pallas kernels, head_step(): pl.pallas_call(functools.partial(head_kernel, devices, float(HEIGHT * WID...  23.3 us
  transfers between devices with their start and end apart: 1, of which 0 were waited for; matrix products, arithmetic and copies ran while one was open for 4% of the time, Pallas kernels for 19%

profile of v3, /device:TPU:0, one launch (start us, length us, event | category | flops | bytes accessed | tf_op | source)
XLA Modules:
  0.0 458.6 jit_solution(13266500878767615459)
XLA Ops:
  7.2 0.0 copy-start.10
  7.2 0.0 copy-start.11
  7.2 0.0 copy-start.12
  7.2 0.0 all-gather.3.cloned.1.call-start
  7.3 1.3 fusion.5.idx_ref
  8.6 1.1 convert_bitcast_fusion
  9.6 92.2 %shard_map.264 = (bf16[4,2048,128]{2,1,0:T(8,128)(2,1)}, bf16[4,4608,128]{2,1,0:T(8,128)(2,1)}, bf16[16,512,128]{2,1,0:T(8,128)(2,1)}, bf16[4,2048,128]{2,1,0:T(...) custom-call(s32[2176]{0:T(1024)} %fusion.5.idx_ref, f32[136,4096]{1,0:T(8,128)} %m_ref.1), custom_call_target="tpu_custom_call" | custom-call | tf_op jit(solution)/shard_map/pallas_call | solution.py:262
  101.9 0.7 pad.8
  102.6 0.0 all-gather.3.cloned.1.call-update
  102.6 0.0 copy-done.10
  102.7 0.1 reshape.191
  102.7 0.1 dynamic_slice.10
  102.8 0.0 copy-done.11
  102.8 0.1 reshape.190
  102.9 0.1 dynamic_slice.9
  103.0 0.0 copy-done.12
  103.0 0.1 and_convert_fusion
  103.1 0.1 broadcast_in_dim.75
  103.2 5.9 %copy.35 = bf16[4,7,32,2048]{3,2,1,0:T(8,128)(2,1)} copy(bf16[4,7,32,2048]{3,0,1,2:T(4,128)(2,1)} %bitcast.33) | data formatting | bytes 7340032 | tf_op jit(solution)/shard_map/transpose | solution.py:1835
  109.1 0.1 mul.117
  109.2 0.1 eq.83
  109.3 0.1 reshape.189
  109.4 0.0 copy-done.13
  109.4 0.1 dynamic_slice.11
  109.4 0.0 slice-done.2
  109.4 0.6 pad.9
  110.0 0.0 copy-done.6
  110.0 0.6 slice_bitcast_fusion.2
  110.7 1.0 broadcast_in_dim.76.refs_9_.refs_28_
  111.6 87.3 %shard_map.265 = (f32[4,896,128]{2,1,0:T(8,128)}, bf16[4,6,9,32,128]{4,3,2,1,0:T(8,128)(2,1)}, f32[4,896,128]{2,1,0:T(8,128)}, bf16[4,896,128]{2,1,0:T(8,128)(2,...) custom-call(bf16[4,2048,128]{2,1,0:T(8,128)(2,1)} %get-tuple-element, ...), custom_call_target="tpu_custom_call" | custom-call | tf_op jit(solution)/shard_map/pallas_call | solution.py:1060
  199.0 0.6 convert_reduce_fusion
  199.6 0.2 select_reduce_fusion.1
  199.8 1.3 select_select_fusion.numbers
  201.1 0.7 compare_convert_fusion.pick
  201.7 0.7 select_convert_fusion.point
  202.4 0.7 fusion.2.hot
  203.1 0.0 copy-done.9
  203.1 0.0 copy-done.14
  203.1 3.3 select_reduce_fusion.code_ref
  206.5 23.3 %shard_map.266 = (f32[16,128]{1,0:T(8,128)}, f32[16,32,128]{2,1,0:T(8,128)}, f32[16,16,128]{2,1,0:T(8,128)}, f32[16,1024]{1,0:T(8,128)}) custom-call(f32[16,32,128]{2,1,0:T(8,128)} %get-tuple-element.76.pooled, bf16[16,1024,128]{2,1,0:T(8,128)(2,1)} %bitcast.32, f32[1,1024]{1,0:T(1,128)} %bitcast.38, bf16[16,512]{1,0:T(8,128)(2,1)} %compare_convert_fusion.pick, ...), custom_call_target="tpu_custom_call" | custom-call | tf_op jit(solution)/shard_map/pallas_call | solution.py:1224
  229.8 110.7 %shard_map.267 = (bf16[256,16,128]{2,1,0:T(8,128)(2,1)}, bf16[576,16,128]{2,1,0:T(8,128)(2,1)}, bf16[256,16,128]{2,1,0:T(8,128)(2,1)}, bf16[256,16,128]{2,1,0:T(...) custom-call(f32[16,896,128]{2,1,0:T(8,128)} %get-tuple-element.64.re, ...), custom_call_target="tpu_custom_call" | custom-call | tf_op jit(solution)/shard_map/pallas_call | solution.py:1738
  340.5 0.7 slice_bitcast_fusion
  341.2 0.7 slice_bitcast_fusion.4
  341.9 1.2 slice.30
  343.1 0.7 slice_bitcast_fusion.1
  343.8 97.8 %shard_map.268 = (bf16[2,32,16,128]{3,2,1,0:T(8,128)(2,1)}, f32[136,4096]{1,0:T(8,128)}, f32[136,64,128]{2,1,0:T(8,128)}, f32[136,4096]{1,0:T(8,128)}) custom-call(s32[2176]{0:T(1024)} %select_reduce_fusion.code_ref, bf16[32,16,128]{2,1,0:T(8,128)(2,1)} %get-tuple-element.89.head_h, bf16[256,16,128]{2,1,0:T(8,128)(2,1)} %get-tuple-element.90.refs_0_, ...), custom_call_target="tpu_custom_call" | custom-call | tf_op jit(solution)/shard_map/pallas_call | solution.py:572
  441.6 0.0 copy-done
  441.6 0.0 copy-start.2
  441.6 0.0 copy-start.3
  441.6 0.0 copy-start.4
  441.6 0.0 copy-start.5
  441.6 0.0 slice-start
  441.6 3.9 fusion.11
  445.5 0.0 copy-done.2
  445.5 0.0 copy-done.3
  445.5 0.0 copy-done.4
  445.5 0.0 slice-start.1
  445.6 1.5 fusion.8
  447.1 0.0 copy-done.8
  447.1 0.7 multiply_subtract_fusion.2
  447.7 0.1 copy-done.1
  447.8 1.4 copy.40
  449.2 0.0 slice-done.1
  449.2 2.1 copy.41
  (23 shorter events, 0.1 us)
Async XLA Ops:
  7.2 95.5 %copy-start.10 = (s32[512]{0:T(512)S(1)}, s32[512]{0:T(512)}, u32[]{:S(2)}) copy-start(s32[512]{0:T(512)} %param.21) | copy-start | bytes 6148
  7.2 95.6 %copy-start.11 = (s32[512]{0:T(512)S(1)}, s32[512]{0:T(512)}, u32[]{:S(2)}) copy-start(s32[512]{0:T(512)} %param.20) | copy-start | bytes 6148
  7.2 95.8 %copy-start.12 = (s32[32]{0:T(128)S(1)}, s32[32]{0:T(128)}, u32[]{:S(2)}) copy-start(s32[32]{0:T(128)} %param.18) | copy-start | bytes 388
  7.2 199.3 %all-gather.3.cloned.1.call-start = ((), (), s32[]{:S(2)}) async-start(), calls=%async_computation | async-start | bytes 4456448 | tf_op jit(solution)/shard_map/all_gather | solution.py:1824
  103.2 6.2 %copy-start.13 = (s32[32]{0:T(128)S(1)}, s32[32]{0:T(128)}, u32[]{:S(2)}) copy-start(s32[32]{0:T(128)} %param.19) | copy-start | bytes 388
  103.2 6.3 %slice-start.2 = ((f32[13288]{0:T(1024)}), f32[1000]{0:T(1024)S(1)}, s32[]{:S(2)}) async-start(f32[13288]{0:T(1024)} %param.29), calls=%async_computation.3 | async-start | bytes 8192 | tf_op jit(solution)/shard_map/slice | solution.py:1840
  103.2 6.9 %copy-start.6 = (f32[13288]{0:T(1024)S(1)}, f32[13288]{0:T(1024)}, u32[]{:S(2)}) copy-start(f32[13288]{0:T(1024)} %param.29) | copy-start | bytes 159460
  111.6 91.5 %copy-start.9 = (s32[2176]{0:T(1024)S(1)}, s32[2176]{0:T(1024)}, u32[]{:S(2)}) copy-start(s32[2176]{0:T(1024)} %param.22) | copy-start | bytes 26116
  111.6 91.5 %copy-start.14 = (s32[2176]{0:T(1024)S(1)}, s32[2176]{0:T(1024)}, u32[]{:S(2)}) copy-start(s32[2176]{0:T(1024)} %constant.103) | copy-start | bytes 26116
  343.8 97.8 %copy-start = (f32[136,4096]{1,0:T(8,128)S(1)}, f32[136,4096]{1,0:T(8,128)}, u32[]{:S(2)}) copy-start(f32[136,4096]{1,0:T(8,128)} %m_ref.1) | copy-start | bytes 6684676
  441.6 3.9 copy-start.2
  441.6 3.9 copy-start.3
  441.6 3.9 copy-start.4
  441.6 3.9 copy-start.5
  441.6 7.6 %slice-start = ((s8[4456448]{0:T(1024)(128)(4,1)}), s8[4194304]{0:T(1024)(128)(4,1)S(1)}, s32[]{:S(2)}) async-start(s8[4456448]{0:T(1024)(128)(4,1)} %bitcast.30), calls=%async_computation.1 | async-start | bytes 8388608
  445.5 1.6 copy-start.7
  445.5 1.6 copy-start.8
  445.5 2.3 copy-start.1
  445.5 3.7 slice-start.1
Sparse Core Ops, SparseCore 0:
  102.7 80.3 all-gather.2
